TPU v7x, 256 devices: a whole 4x4x8 slice. The times are simulated.
256 devices in a mesh: sector: 8 (over z), rows: 32 (over x, y, core).
Axes of the slice: x: 4, y: 4, z: 8, core: 2. Of those that a mesh axis runs over, the one named last changes fastest.
Arguments:
- x_block: bfloat16 [8, 40960, 300], P('sector', 'rows')
- h_diag: bfloat16 [8, 40960, 1280], P('sector', 'rows')
- h_right: bfloat16 [8, 40960, 1280], P('sector', 'rows')
- pattern: int32 [8, 2, 320, 10], P('sector', None, 'rows'), may hold values from 0 to 1, as said below
Outputs:
- q_block: bfloat16 [8, 40960, 300], P('sector', 'rows')
- hproj: float32 [8, 300, 300], P('sector')
- correlation: float32 [8, 300, 300], P('sector')
Inputs may be any that keep to these rules, and one draw needn't show every extreme that they name: Within each 1280 x 1280 tile, pattern[s, 0] is symmetric with ones on its diagonal; h_diag's tiles are symmetric.
All inputs are finite; a program needn't handle non-finite values.
Results may differ from a plain program's by a relative error of at most 0.011.
Values may be sent and summed in bfloat16 or wider, within the bound.
A program may use at most 64 MiB of HBM per device.

v0:
```python
import jax
import jax.numpy as jnp
from jax import lax
from jax.sharding import PartitionSpec as P

SUBBLOCK = 128


def from_behind(value, axis, steps):
    count = lax.axis_size(axis)
    leading, last = (max(0, -steps), min(count, count - steps))
    return lax.ppermute(value, axis, [(source, source + steps) for source in range(leading, last)])


def column_product(left, right):
    return lax.dot_general(
        left, right, (((0,), (0,)), ((), ())), preferred_element_type=jnp.float32
    )


def expand(blocks):
    return jnp.repeat(jnp.repeat(blocks, SUBBLOCK, axis=0), SUBBLOCK, axis=1)


def apply_factor(rows_b, inverse):
    return jnp.dot(rows_b.astype(jnp.float32), inverse.T, precision=lax.Precision.HIGH).astype(
        jnp.bfloat16
    )


def shards(x_block, h_diag, h_right, pattern):
    inputs = x_block[0]
    masks = pattern[0].astype(jnp.bfloat16)
    diag_tile = h_diag[0] * expand(masks[0])
    right_tile = h_right[0] * expand(masks[1])
    later_rows = from_behind(inputs, "rows", -1)
    carried = column_product(right_tile, inputs)
    earlier = from_behind(carried.astype(jnp.bfloat16), "rows", 1).astype(carried.dtype)
    image = jnp.dot(diag_tile, inputs, preferred_element_type=jnp.float32)
    image = image + jnp.dot(right_tile, later_rows, preferred_element_type=jnp.float32) + earlier
    image_b = image.astype(jnp.bfloat16)
    total_rows = lax.axis_size("rows") * inputs.shape[0]
    gram, rayleigh = lax.psum(
        (column_product(image_b, image_b), column_product(inputs, image_b)), "rows"
    )
    gram = gram / total_rows
    rayleigh = rayleigh / total_rows
    factor = jnp.linalg.cholesky(gram)
    inverse = jax.scipy.linalg.solve_triangular(
        factor, jnp.eye(gram.shape[0], dtype=jnp.float32), lower=True
    )
    basis = apply_factor(image_b, inverse)
    previous = from_behind(basis, "sector", 1)
    correlation = (
        lax.psum(column_product(previous, basis).astype(jnp.bfloat16), "rows").astype(jnp.float32)
        / total_rows
    )
    return (basis[None], rayleigh[None], correlation[None])


def solution(mesh):
    in_specs = (
        P("sector", "rows", None),
        P("sector", "rows", None),
        P("sector", "rows", None),
        P("sector", None, "rows", None),
    )
    out_specs = (P("sector", "rows", None), P("sector", None, None), P("sector", None, None))
    return jax.shard_map(shards, mesh=mesh, in_specs=in_specs, out_specs=out_specs, check_vma=False)
```

profile of v0, /device:TPU:97, one launch (start us, length us, event | category | flops | bytes accessed | tf_op | source)
XLA Modules:
  0.0 390.9 jit_solution(5937771413376753806)
XLA Ops:
  7.2 0.7 copy_convert_fusion
  8.2 4.0 %copy.16 = bf16[1,1280,1280]{1,2,0:T(8,128)(2,1)S(1)} copy(bf16[1,1280,1280]{2,1,0:T(8,128)(2,1)} %param.6) | data formatting | bytes 6553600 | tf_op args[2]
  12.2 0.2 bitcast_multiply_fusion
  12.4 3.2 fusion.6
  15.6 3.8 collective-permute-start.1
  19.4 1.9 collective-permute-start
  21.3 1.9 bitcast_multiply_fusion.1
  23.5 4.0 %copy.15 = bf16[1,1280,1280]{1,2,0:T(8,128)(2,1)S(1)} copy(bf16[1,1280,1280]{2,1,0:T(8,128)(2,1)} %param.5) | data formatting | bytes 6553600 | tf_op args[1]
  27.5 0.2 bitcast_multiply_fusion.2
  27.8 2.5 fusion.2
  30.3 2.7 collective-permute-done
  33.0 2.7 fusion.5
  35.6 2.5 convolution_bitcast_fusion
  38.1 1.4 fusion.39
  39.5 0.2 all-reduce.7.cloned.1.call-start
  39.9 117.2 %all-reduce.9.cloned.1.call-done = (f32[300,300]{0,1:T(8,128)}, f32[300,300]{0,1:T(8,128)}) async-done(((f32[300,300]{0,1:T(8,128)}, f32[300,300]{0,1:T(8,128)}), (f32[300,300]{0,1:T(8,128)}, f32[300,300]{0,1:T(8,128)})) %all-reduce.9.cloned.1.call-update) | async-done | bytes 720016 | tf_op jit(solution)/shard_map/psum | solution.py:43
  157.1 1.1 broadcast_multiply_fusion
  158.2 0.2 copy.20
  158.4 1.1 fusion.14
  159.5 11.7 %cholesky.78 = f32[128,128]{1,0:T(8,128)S(1)} custom-call(f32[128,128]{1,0:T(8,128)S(1)} %cholesky.198), custom_call_target="Cholesky" | custom-call | tf_op jit(solution)/shard_map/jit(cholesky)/cholesky | solution.py:48
  171.2 9.8 %custom-call.23 = f32[1,128,128]{1,2,0:T(8,128)S(1)} custom-call(f32[1,128,128]{2,1,0:T(8,128)S(1)} %get-tuple-element.33), custom_call_target="InvertDiagBlocksLowerTriangular" | custom-call | tf_op jit(solution)/shard_map/jit(cholesky)/cholesky | solution.py:48
  181.1 0.2 constant_dynamic-update-slice_fusion.2
  181.3 0.3 convolution_subtract_fusion.1
  181.6 11.7 %cholesky.164 = f32[128,128]{1,0:T(8,128)S(1)} custom-call(f32[128,128]{1,0:T(8,128)S(1)} %cholesky.202), custom_call_target="Cholesky" | custom-call | tf_op jit(solution)/shard_map/jit(cholesky)/cholesky | solution.py:48
  193.4 10.0 %custom-call.24 = f32[1,128,128]{1,2,0:T(8,128)S(1)} custom-call(f32[1,128,128]{2,1,0:T(8,128)S(1)} %get-tuple-element.30), custom_call_target="InvertDiagBlocksLowerTriangular" | custom-call | tf_op jit(solution)/shard_map/jit(cholesky)/cholesky | solution.py:48
  203.5 0.2 convolution_subtract_fusion.3
  203.7 4.0 %cholesky.186 = f32[44,44]{1,0:T(8,128)S(1)} custom-call(f32[44,44]{1,0:T(8,128)S(1)} %convolution_subtract_fusion.3), custom_call_target="Cholesky" | custom-call | tf_op jit(solution)/shard_map/jit(cholesky)/cholesky | solution.py:48
  207.8 0.6 compare_reduce_fusion
  208.4 0.6 compare_reduce_fusion.1
  211.1 4.0 %while.1 = (s32[]{:T(128)}, f32[300,300]{1,0:T(8,128)S(1)}, s32[2,2]{1,0:T(2,128)S(1)}, f32[2,128,128]{2,1,0:T(8,128)S(1)}, s32[]{:T(128)}) while((s32[]{:T(128)}, f32[300,300]{1,0:T(8,128)S(1)}, s32[2,2]{1,0:T(2,128)S(1)}, f32[2,128,128]{2,1,0:T(8,128)S(1)}, s32[]{:T(128)}) %tuple.32), condition=%wide.while_cond, body=%wide.while_body.sunk | while | flops 2 | bytes 131181 | solution.py:49
  211.1 0.6 fusion.53
  211.7 1.4 bitcast_dynamic-update-slice_fusion.2
  213.1 0.6 fusion.53
  213.7 1.4 bitcast_dynamic-update-slice_fusion.2
  215.3 29.5 %custom-call.25 = f32[3,128,128]{1,2,0:T(8,128)S(1)} custom-call(f32[3,128,128]{2,1,0:T(8,128)S(1)} %pad_maximum_fusion), custom_call_target="InvertDiagBlocksLowerTriangular" | custom-call | tf_op jit(solution)/shard_map/jit(_solve_triangular)/triangular_solve | solution.py:49
  244.8 0.3 fusion.18
  245.1 0.3 convolution_subtract_fusion
  245.4 0.5 fusion.24
  245.9 0.4 convolution_subtract_fusion.2
  246.3 0.4 fusion.31
  246.8 1.0 convolution_convert_fusion
  247.8 4.4 %collective-permute-start.2 = (bf16[1280,300]{0,1:T(8,128)(2,1)S(1)}, bf16[1280,300]{0,1:T(8,128)(2,1)S(1)}, u32[]{:S(2)}, u32[]{:S(2)}) collective-permute-start(bf16[1280,300]{0,1:T(8,128)(2,1)S(1)} %convolution_convert_fusion), channel_id=1, source_target_pairs={{0,32},{32,64},{64,96},{96,128},{128,160},{160,192},{192,224},{1,3... | collective-permute-start | bytes 2304008 | tf_op jit(solution)/shard_map/ppermute | solution.py:12
  252.2 16.4 %collective-permute-done.2 = bf16[1280,300]{0,1:T(8,128)(2,1)S(1)} collective-permute-done((bf16[1280,300]{0,1:T(8,128)(2,1)S(1)}, bf16[1280,300]{0,1:T(8,128)(2,1)S(1)}, u32[]{:S(2)}, u32[]{:S(2)}) %collective-permute-start.2) | collective-permute-done | bytes 768032 | tf_op jit(solution)/shard_map/ppermute | solution.py:12
  268.6 1.3 convolution_convert_fusion.1
  270.0 1.2 copy.22
  271.1 110.7 %all-reduce.7.cloned.1.call-done = bf16[300,300]{0,1:T(8,128)(2,1)} async-done(((bf16[300,300]{0,1:T(8,128)(2,1)}), bf16[300,300]{0,1:T(8,128)(2,1)}) %all-reduce.7.cloned.1.call-update) | async-done | bytes 180016 | tf_op jit(solution)/shard_map/psum | solution.py:55
  381.9 1.0 multiply_bitcast_fusion
  382.9 1.2 copy.23
  (40 shorter events, 1.2 us)
Async XLA Ops:
  7.2 149.9 %all-reduce.9.cloned.1.call-start = ((), (), s32[]{:S(2)}) async-start(), calls=%async_computation.1 | async-start | bytes 1867776 | tf_op jit(solution)/shard_map/psum | solution.py:43
  15.6 14.6 %collective-permute-start.1 = (bf16[1280,300]{0,1:T(8,128)(2,1)}, bf16[1280,300]{0,1:T(8,128)(2,1)}, u32[]{:S(2)}, u32[]{:S(2)}) collective-permute-start(bf16[1280,300]{0,1:T(8,128)(2,1)} %fusion.6), channel_id=1, source_target_pairs={{0,1},{1,2},{2,3},{3,4},{4,5},{5,6},{6,7},{7,8},{8,9},{9,10},{10,1... | collective-permute-start | bytes 2304008 | tf_op jit(solution)/shard_map/ppermute | solution.py:12
  19.4 13.5 %collective-permute-start = (bf16[1280,300]{0,1:T(8,128)(2,1)}, bf16[1280,300]{0,1:T(8,128)(2,1)}, u32[]{:S(2)}, u32[]{:S(2)}) collective-permute-start(bf16[1280,300]{0,1:T(8,128)(2,1)} %bitcast.3), channel_id=1, source_target_pairs={{1,0},{2,1},{3,2},{4,3},{5,4},{6,5},{7,6},{8,7},{9,8},{10,9},{11,1... | collective-permute-start | bytes 2304008 | tf_op jit(solution)/shard_map/ppermute | solution.py:12
  27.8 5.2 %copy-start = (bf16[1280,1280]{0,1:T(8,128)(2,1)S(1)}, bf16[1280,1280]{0,1:T(8,128)(2,1)}, u32[]{:S(2)}) copy-start(bf16[1280,1280]{0,1:T(8,128)(2,1)} %bitcast_multiply_fusion.1) | copy-start | bytes 9830404
  39.5 342.4 %all-reduce.7.cloned.1.call-start = ((), (), s32[]{:S(2)}) async-start(), calls=%async_computation | async-start | bytes 466944 | tf_op jit(solution)/shard_map/psum | solution.py:55
  215.2 54.7 %copy-start.2 = (f32[300,300]{0,1:T(8,128)S(1)}, f32[300,300]{0,1:T(8,128)}, u32[]{:S(2)}) copy-start(f32[300,300]{0,1:T(8,128)} %get-tuple-element.26) | copy-start | bytes 1080004
  247.8 136.2 %copy-start.1 = (bf16[1280,300]{0,1:T(8,128)(2,1)}, bf16[1280,300]{0,1:T(8,128)(2,1)S(1)}, u32[]{:S(2)}) copy-start(bf16[1280,300]{0,1:T(8,128)(2,1)S(1)} %convolution_convert_fusion) | copy-start | bytes 2304004
  247.8 20.8 %collective-permute-start.2 = (bf16[1280,300]{0,1:T(8,128)(2,1)S(1)}, bf16[1280,300]{0,1:T(8,128)(2,1)S(1)}, u32[]{:S(2)}, u32[]{:S(2)}) collective-permute-start(bf16[1280,300]{0,1:T(8,128)(2,1)S(1)} %convolution_convert_fusion), channel_id=1, source_target_pairs={{0,32},{32,64},{64,96},{96,128},{128,160},{160,192},{192,224},{1,3... | collective-permute-start | bytes 2304008 | tf_op jit(solution)/shard_map/ppermute | solution.py:12
Sparse Core Ops, SparseCore 0:
  39.6 117.4 all-reduce.8
  270.0 111.8 all-reduce.6
where the time goes:
time: 393 us; the launch traced here: 391 us
  waiting for transfers between devices  247 us (63%)
  other arithmetic  84.6 us (22%)
  matrix products  17.4 us (4%)
  between operations  16.4 us (4%)
  local copies, waits for them, and re-layouts  15.1 us (4%)
  starting transfers between devices  10.3 us (3%)
    psum x1, waiting for transfers between devices, shards(): lax.psum((column_product(image_b, image_b), column_product(inputs, image_...  117 us
    psum x1, waiting for transfers between devices, shards(): lax.psum(column_product(previous, basis).astype(jnp.bfloat16), 'rows')  111 us
    another operation x10, other arithmetic, shards(): factor = jnp.linalg.cholesky(gram)  48.6 us
    another operation x7, other arithmetic, shards(): jax.scipy.linalg.solve_triangular(factor, jnp.eye(gram.shape[0], dtype=jn...  29.7 us
    ppermute x3, waiting for transfers between devices, from_behind(): lax.ppermute(value, axis, [(source, source + steps) for source in range(l...  19 us
    unnamed x16, local copies, waits for them, and re-layouts  10.7 us
    ppermute x3, starting transfers between devices, from_behind(): lax.ppermute(value, axis, [(source, source + steps) for source in range(l...  10.1 us
    dot_general x4, matrix products, column_product(): lax.dot_general(left, right, (((0,), (0,)), ((), ())), preferred_element_...  8.35 us
  transfers between devices with their start and end apart: 5, of which 4 were waited for; matrix products, arithmetic and copies ran while one was open for 3% of the time, Pallas kernels for 0%

commit v1 on v0

v1 whole, which is shorter than its diff:
```python
import jax
import jax.numpy as jnp
from jax import lax
from jax.experimental import pallas as pl
from jax.experimental.pallas import tpu as pltpu
from jax.sharding import PartitionSpec as P

HI = lax.Precision.HIGHEST
MESH = pl.DeviceIdType.MESH
F32 = jnp.float32
BF16 = jnp.bfloat16
N = 304
LANES = 384
C = 300
ROWS = 1280
CHUNK = 256
NCH = ROWS // CHUNK
BLOCK = 128


def nt(a, b, precision=None):
    return lax.dot_general(a, b, (((1,), (1,)), ((), ())), precision=precision, preferred_element_type=F32)


def tn(a, b, precision=None):
    return lax.dot_general(a, b, (((0,), (0,)), ((), ())), precision=precision, preferred_element_type=F32)


def nn(a, b, precision=None):
    return lax.dot_general(a, b, (((1,), (0,)), ((), ())), precision=precision, preferred_element_type=F32)


def panel_block(tiles, base_lane, count):
    lane = lax.broadcasted_iota(jnp.int32, (8, 128), 1)
    sub = lax.broadcasted_iota(jnp.int32, (8, 128), 0)
    ntile = len(tiles[0])
    for k in range(count):
        lo = 8 * k
        inside = (lane >= lo) & (lane < lo + 8)
        P = tiles[k]
        rows = [[jnp.broadcast_to(P[t][q:q + 1, :], (8, 128)) for t in range(ntile)] for q in range(8)]
        s = [[jnp.broadcast_to(rows[q][0][:, lo + p:lo + p + 1], (8, 128)) if p >= q else None for p in range(8)] for q in range(8)]
        for q in range(8):
            rows[q][0] = jnp.where(inside, jnp.where(lane == lo + q, 1.0, 0.0), rows[q][0])
        u = [[None] * 8 for _ in range(8)]
        rs = [None] * 8
        for p in range(8):
            rs[p] = lax.rsqrt(s[p][p])
            for r in range(p + 1, 8):
                u[p][r] = s[p][r] * rs[p]
            for q in range(p + 1, 8):
                for r in range(q, 8):
                    s[q][r] = s[q][r] - u[p][q] * u[p][r]
            rows[p] = [x * rs[p] for x in rows[p]]
            for q in range(p + 1, 8):
                rows[q] = [x - u[p][q] * y for x, y in zip(rows[q], rows[p])]
        fin = []
        for t in range(ntile):
            acc = rows[0][t]
            for q in range(1, 8):
                acc = jnp.where(sub == q, rows[q][t], acc)
            fin.append(acc)
        tiles[k] = fin
        for g in range(k + 1, count):
            cols = []
            for p in range(8):
                c = jnp.broadcast_to(tiles[g][0][:, lo + p:lo + p + 1], (8, 128))
                for q in range(p):
                    c = c - cols[q] * u[q][p]
                cols.append(c * rs[p])
            new = list(tiles[g])
            new[0] = jnp.where(inside, 0.0, new[0])
            for t in range(ntile):
                acc = new[t]
                for p in range(8):
                    acc = acc - cols[p] * rows[p][t]
                new[t] = acc
            tiles[g] = new
    return tiles

def chol_body(w):
    lane3 = None
    for b, cnt in ((0, 16), (1, 16), (2, 6)):
        r0 = 128 * b
        order = [b] + [t for t in range(3) if t != b]
        tiles = [[w[t, r0 + 8 * g:r0 + 8 * g + 8, :] for t in order] for g in range(cnt)]
        tiles = panel_block(tiles, r0, cnt)
        for g in range(cnt):
            for i, t in enumerate(order):
                w[t, r0 + 8 * g:r0 + 8 * g + 8, :] = tiles[g][i]
        r1 = r0 + 8 * cnt
        if r1 < N:
            m = N - r1
            left = jnp.concatenate([w[t, r0:r1, :] for t in range(b + 1, 3)], axis=1)[:, :]
            for t in range(3):
                right = w[t, r0:r1, :]
                if t == b:
                    size = r1 - r0
                    right = jnp.where(lax.broadcasted_iota(jnp.int32, (size, 128), 1) <= lax.broadcasted_iota(jnp.int32, (size, 128), 0), right, 0.0)
                upd = lax.dot_general(left, right, (((0,), (0,)), ((), ())), precision=HI, preferred_element_type=jnp.float32)[:m]
                if t == b:
                    w[t, r1:N, :] = -upd
                else:
                    w[t, r1:N, :] = w[t, r1:N, :] - upd


def iota(shape, dim):
    return lax.broadcasted_iota(jnp.int32, shape, dim)


def pack_symmetric(full, out):
    corner = pltpu.roll(full[256:304, 256:384], 0, 1)
    out[0:80, :] = full[0:80, 0:128]
    low = full[80:128, 0:128]
    out[80:128, :] = jnp.where(iota((48, 128), 1) < 48, corner, low)
    out[128:256, :] = full[0:128, 128:256]
    out[256:384, :] = full[128:256, 128:256]
    out[384:512, :] = full[0:128, 256:384] + pltpu.roll(full[128:256, 256:384], 64, 1)


def unpack_upper(packed):
    top = packed[0:128, :]
    upper = iota((128, 128), 1) >= iota((128, 128), 0)
    b00 = jnp.where(upper, top, top.T)
    b22 = jnp.where(iota((48, 128), 1) < 44, top[80:128, :], 0.0)
    both = packed[384:512, :]
    left = iota((128, 128), 1) < 64
    b02 = jnp.where(left, both, 0.0)
    b12 = jnp.where(left, pltpu.roll(both, 64, 1), 0.0)
    return b00, packed[128:256, :], packed[256:384, :], b02, b12, b22


def exchange_sum(me, sector, count, part, recv, total, sems, scale):
    send, arrive, send2, arrive2 = sems
    size = part.shape[0] // count

    def rows_of(index):
        return pl.ds(pl.multiple_of(index * size, 8), size)

    def first(k):
        peer = lax.rem(me + k, count)
        return pltpu.make_async_remote_copy(
            src_ref=part.at[rows_of(peer)], dst_ref=recv.at[k], send_sem=send.at[k], recv_sem=arrive.at[k],
            device_id=(sector, peer), device_id_type=MESH)

    def second(k):
        peer = lax.rem(me + k, count)
        return pltpu.make_async_remote_copy(
            src_ref=total.at[rows_of(me)], dst_ref=total.at[rows_of(me)], send_sem=send2.at[k],
            recv_sem=arrive2.at[k], device_id=(sector, peer), device_id_type=MESH)

    def start1(k, carry):
        first(k).start()
        return carry

    def sum1(k, acc):
        first(k).wait_recv()
        return acc + recv[k]

    def start2(k, carry):
        second(k).start()
        return carry

    def wait2(k, carry):
        second(k).wait_recv()
        return carry

    def drain(k, carry):
        first(k).wait_send()
        second(k).wait_send()
        return carry

    lax.fori_loop(1, count, start1, 0)
    acc = lax.fori_loop(1, count, sum1, part[rows_of(me), :])
    total[rows_of(me), :] = acc * scale
    lax.fori_loop(1, count, start2, 0)
    return lambda: (lax.fori_loop(1, count, wait2, 0), lax.fori_loop(1, count, drain, 0))


def greet(me, sector, count):
    barrier = pltpu.get_barrier_semaphore()

    def signal(k, carry):
        pl.semaphore_signal(barrier, inc=1, device_id=(sector, lax.rem(me + k, count)), device_id_type=MESH)
        return carry

    lax.fori_loop(1, count, signal, 0)
    return barrier


def front_kernel(count, pattern, x_hbm, d_hbm, r_hbm, y_out, s_out,
                 xv, xn, dv, rv, acc, cs, cr, full, part, recv, total,
                 load, xsend, xrecv, csend, crecv, s1, s2, s3, s4):
    me = lax.axis_index("rows")
    sector = lax.axis_index("sector")
    loads = [pltpu.make_async_copy(x_hbm, xv, load.at[0])]
    for c in range(NCH):
        cols = pl.ds(c * CHUNK, CHUNK)
        loads.append(pltpu.make_async_copy(r_hbm.at[:, cols], rv.at[:, cols], load.at[1 + c]))
    for c in range(NCH):
        cols = pl.ds(c * CHUNK, CHUNK)
        loads.append(pltpu.make_async_copy(d_hbm.at[:, cols], dv.at[:, cols], load.at[1 + NCH + c]))
    for l in loads:
        l.start()
    barrier = greet(me, sector, count)
    pl.semaphore_wait(barrier, count - 1)

    def x_copy(c):
        cols = pl.ds(c * CHUNK, CHUNK)
        return pltpu.make_async_remote_copy(
            src_ref=x_hbm.at[:, cols], dst_ref=xn.at[:, cols], send_sem=xsend.at[c], recv_sem=xrecv.at[c],
            device_id=(sector, me - 1), device_id_type=MESH)

    def c_copy(c):
        cols = pl.ds(c * CHUNK, CHUNK)
        return pltpu.make_async_remote_copy(
            src_ref=cs.at[:, cols], dst_ref=cr.at[:, cols], send_sem=csend.at[c], recv_sem=crecv.at[c],
            device_id=(sector, me + 1), device_id_type=MESH)

    @pl.when(me > 0)
    def _():
        for c in range(NCH):
            x_copy(c).start()

    full[...] = jnp.zeros((N, LANES), F32)

    def mask(tile, which, c):
        for i in range(ROWS // BLOCK):
            for j in range(CHUNK // BLOCK):
                row = slice(i * BLOCK, (i + 1) * BLOCK)
                col = slice(c * CHUNK + j * BLOCK, c * CHUNK + (j + 1) * BLOCK)
                keep = pattern[i, which, c * (CHUNK // BLOCK) + j]
                scale = jnp.full((BLOCK, BLOCK), keep.astype(F32)).astype(BF16)
                tile[row, col] = tile[row, col] * scale

    loads[0].wait()
    for c in range(NCH):
        cols = slice(c * CHUNK, (c + 1) * CHUNK)
        loads[1 + c].wait()
        mask(rv, 1, c)
        cs[:, cols] = nn(xv[...], rv[:, cols]).astype(BF16)

        @pl.when(me < count - 1)
        def _():
            c_copy(c).start()

    for c in range(NCH):
        cols = slice(c * CHUNK, (c + 1) * CHUNK)
        loads[1 + NCH + c].wait()
        mask(dv, 0, c)
        acc[:, cols] = nn(xv[...], dv[:, cols])

    for c in range(NCH):
        @pl.when(me < count - 1)
        def _():
            cols = slice(c * CHUNK, (c + 1) * CHUNK)
            x_copy(c).wait_recv()
            for j in range(NCH):
                out = slice(j * CHUNK, (j + 1) * CHUNK)
                acc[:, out] += nt(xn[:, cols], rv[out, cols])

    gram = None
    for c in range(NCH):
        cols = slice(c * CHUNK, (c + 1) * CHUNK)

        @pl.when(me > 0)
        def _():
            c_copy(c).wait_recv()
            acc[:, cols] += cr[:, cols].astype(F32)

        y = acc[:, cols].astype(BF16)
        y_out[:, cols] = y
        g = nt(y, y)
        gram = g if gram is None else gram + g
    full[0:C, 0:C] = gram
    pack_symmetric(full, part)
    finish = exchange_sum(me, sector, count, part, recv, total, (s1, s2, s3, s4), 1.0 / (count * ROWS))

    for c in range(NCH):
        @pl.when(me > 0)
        def _():
            x_copy(c).wait_send()

        @pl.when(me < count - 1)
        def _():
            c_copy(c).wait_send()

    finish()
    b00, b01, b11, b02, b12, b22 = unpack_upper(total)
    s_out[...] = jnp.zeros((3, N, BLOCK), F32)
    s_out[0, 0:128, :] = b00
    s_out[1, 0:128, :] = b01
    s_out[2, 0:128, :] = b02
    s_out[1, 128:256, :] = b11
    s_out[2, 128:256, :] = b12
    extra = (iota((48, 128), 0) == iota((48, 128), 1)) & (iota((48, 128), 0) >= 44)
    s_out[2, 256:304, :] = jnp.where(extra, 1.0, b22)


def front(count, pattern, x, d, r):
    dma = pltpu.SemaphoreType.DMA
    return pl.pallas_call(
        lambda *refs: front_kernel(count, *refs),
        out_shape=(jax.ShapeDtypeStruct((C, ROWS), BF16), jax.ShapeDtypeStruct((3, N, BLOCK), F32)),
        in_specs=[pl.BlockSpec(memory_space=pltpu.SMEM)] + [pl.BlockSpec(memory_space=pl.ANY)] * 3,
        out_specs=(pl.BlockSpec(memory_space=pltpu.VMEM),) * 2,
        scratch_shapes=[
            pltpu.VMEM((C, ROWS), BF16), pltpu.VMEM((C, ROWS), BF16),
            pltpu.VMEM((ROWS, ROWS), BF16), pltpu.VMEM((ROWS, ROWS), BF16),
            pltpu.VMEM((C, ROWS), F32), pltpu.VMEM((C, ROWS), BF16), pltpu.VMEM((C, ROWS), BF16),
            pltpu.VMEM((N, LANES), F32), pltpu.VMEM((512, BLOCK), F32),
            pltpu.VMEM((count, 512 // count, BLOCK), F32), pltpu.VMEM((512, BLOCK), F32),
            dma((1 + 2 * NCH,)), dma((NCH,)), dma((NCH,)), dma((NCH,)), dma((NCH,)),
            dma((count,)), dma((count,)), dma((count,)), dma((count,)),
        ],
        compiler_params=pltpu.CompilerParams(collective_id=0, has_side_effects=True, vmem_limit_bytes=60 << 20),
        name="front",
    )(pattern, x, d, r)


def factor_kernel(s_ref, o_ref, w):
    w[...] = s_ref[...]
    chol_body(w)
    for t in range(3):
        keep = iota((N, BLOCK), 1) + BLOCK * t <= iota((N, BLOCK), 0)
        o_ref[:, BLOCK * t:BLOCK * (t + 1)] = jnp.where(keep, w[t], 0.0)


def factor(s):
    vmem = pl.BlockSpec(memory_space=pltpu.VMEM)
    return pl.pallas_call(
        factor_kernel, out_shape=jax.ShapeDtypeStruct((N, LANES), F32), in_specs=[vmem], out_specs=vmem,
        scratch_shapes=[pltpu.VMEM((3, N, BLOCK), F32)],
        compiler_params=pltpu.CompilerParams(vmem_limit_bytes=16 << 20), name="factor",
        cost_estimate=pl.CostEstimate(flops=10**10, bytes_accessed=10**6, transcendentals=0),
    )(s)


SYM = 512
CROSS = 768


def split(value):
    high = value.astype(BF16)
    return high, (value - high.astype(F32)).astype(BF16)


def tail_kernel(count, sectors, x, y, yp, linv, q_out, h_out, c_out,
                full, part, recv, total, linvp, lsend, lrecv, s1, s2, s3, s4):
    me = lax.axis_index("rows")
    sector = lax.axis_index("sector")
    linvp[...] = jnp.zeros((N, LANES), F32)
    barrier = greet(me, sector, count)

    @pl.when(sector > 0)
    def _():
        pl.semaphore_signal(barrier, inc=1, device_id=(sector - 1, me), device_id_type=MESH)

    @pl.when(sector < sectors - 1)
    def _():
        pl.semaphore_signal(barrier, inc=1, device_id=(sector + 1, me), device_id_type=MESH)

    full[...] = jnp.zeros((N, LANES), F32)
    full[0:C, 0:C] = nt(x[...], y[...])
    pack_symmetric(full, part)
    full[0:C, 0:C] = nt(yp[...], y[...])
    part[SYM:SYM + N, :] = full[:, 0:128]
    part[SYM + N:SYM + 2 * N, :] = full[:, 128:256]
    part[SYM + 2 * N:SYM + 2 * N + 152, :] = full[0:152, 256:384] + pltpu.roll(full[152:304, 256:384], 64, 1)
    part[SYM + 2 * N + 152:SYM + CROSS, :] = jnp.zeros((8, BLOCK), F32)

    both = jnp.where((sector > 0) & (sector < sectors - 1), 2, 1)
    pl.semaphore_wait(barrier, count - 1 + both)

    def l_copy(b, start, stop):
        piece = (pl.ds(start, stop - start), pl.ds(0, BLOCK * (b + 1)))
        return pltpu.make_async_remote_copy(
            src_ref=linv.at[piece], dst_ref=linvp.at[piece], send_sem=lsend.at[b], recv_sem=lrecv.at[b],
            device_id=(sector + 1, me), device_id_type=MESH)

    spans = ((0, 0, 128), (1, 128, 256), (2, 256, 304))

    @pl.when(sector < sectors - 1)
    def _():
        for span in spans:
            l_copy(*span).start()

    finish = exchange_sum(me, sector, count, part, recv, total, (s1, s2, s3, s4), 1.0 / (count * ROWS))
    high, low = split(linv[...])
    for c in range(NCH):
        cols = slice(c * CHUNK, (c + 1) * CHUNK)
        block = y[:, cols]
        q_out[:, cols] = (nn(high[0:C, 0:C], block) + nn(low[0:C, 0:C], block)).astype(BF16)
    finish()
    b00, b01, b11, b02, b12, b22 = unpack_upper(total)
    h_out[0:128, 0:128] = b00
    h_out[0:128, 128:256] = b01
    h_out[0:128, 256:C] = b02[:, 0:44]
    h_out[128:256, 0:128] = b01.T
    h_out[128:256, 128:256] = b11
    h_out[128:256, 256:C] = b12[:, 0:44]
    h_out[256:C, 0:128] = b02.T[0:44]
    h_out[256:C, 128:256] = b12.T[0:44]
    h_out[256:C, 256:C] = b22[0:44, 0:44]
    full[:, 0:128] = total[SYM:SYM + N, :]
    full[:, 128:256] = total[SYM + N:SYM + 2 * N, :]
    last = total[SYM + 2 * N:SYM + 2 * N + 152, :]
    left = iota((152, BLOCK), 1) < 64
    full[0:152, 256:384] = jnp.where(left, last, 0.0)
    full[152:304, 256:384] = jnp.where(left, pltpu.roll(last, 64, 1), 0.0)
    right = nt(full[...], linv[...], HI)

    @pl.when(sector > 0)
    def _():
        for span in spans:
            l_copy(*span).wait_recv()

    c_out[...] = nn(linvp[:, 0:N], right, HI)[0:C, 0:C]

    @pl.when(sector < sectors - 1)
    def _():
        for span in spans:
            l_copy(*span).wait_send()


def tail(count, sectors, x, y, yp, linv):
    dma = pltpu.SemaphoreType.DMA
    vmem = pl.BlockSpec(memory_space=pltpu.VMEM)
    size = SYM + CROSS
    return pl.pallas_call(
        lambda *refs: tail_kernel(count, sectors, *refs),
        out_shape=(jax.ShapeDtypeStruct((C, ROWS), BF16), jax.ShapeDtypeStruct((C, C), F32),
                   jax.ShapeDtypeStruct((C, C), F32)),
        in_specs=[vmem] * 4, out_specs=(vmem,) * 3,
        scratch_shapes=[
            pltpu.VMEM((N, LANES), F32), pltpu.VMEM((size, BLOCK), F32),
            pltpu.VMEM((count, size // count, BLOCK), F32), pltpu.VMEM((size, BLOCK), F32),
            pltpu.VMEM((N, LANES), F32), dma((3,)), dma((3,)),
            dma((count,)), dma((count,)), dma((count,)), dma((count,)),
        ],
        compiler_params=pltpu.CompilerParams(collective_id=1, has_side_effects=True, vmem_limit_bytes=40 << 20),
        name="tail",
    )(x, y, yp, linv)


def shards(x_block, h_diag, h_right, pattern):
    count, sectors = lax.axis_size("rows"), lax.axis_size("sector")
    x = x_block[0].T
    y, s = front(count, jnp.swapaxes(pattern[0], 0, 1), x, h_diag[0], h_right[0])
    yp = lax.ppermute(y, "sector", [(i, i + 1) for i in range(sectors - 1)])
    linv = factor(s)
    q, h, corr = tail(count, sectors, x, y, yp, linv)
    return q.T[None], h[None], corr[None]


def solution(mesh):
    in_specs = (
        P("sector", "rows", None),
        P("sector", "rows", None),
        P("sector", "rows", None),
        P("sector", None, "rows", None),
    )
    out_specs = (P("sector", "rows", None), P("sector", None, None), P("sector", None, None))
    return jax.shard_map(shards, mesh=mesh, in_specs=in_specs, out_specs=out_specs, check_vma=False)
```

time: 393 us -> 89.9 us (0.23)
  waiting for transfers between devices: 247 us -> 3.96 us
  other arithmetic: 84.6 us -> 0 us
  Pallas kernels: 0 us -> 74.6 us
  matrix products: 17.4 us -> 0 us
  between operations: 16.4 us -> 0.67 us
  local copies, waits for them, and re-layouts: 15.1 us -> 4.38 us
  starting transfers between devices: 10.3 us -> 4.93 us
    psum x2 -> x0, waiting for transfers between devices: 228 us -> none  [the longest x1 117 us: shards(): lax.psum((column_product(image_b, image_b), column_product(inputs, image_...]
    another operation x17 -> x0, other arithmetic: 78.3 us -> none  [the longest x10 48.6 us: shards(): factor = jnp.linalg.cholesky(gram)]
    pallas_call x0 -> x3, Pallas kernels: none -> 74.6 us  [the longest x1 34.8 us: front(): pl.pallas_call(lambda *refs: front_kernel(count, *refs), out_shape=(jax.S...]
    ppermute x3 -> x1, waiting for transfers between devices: 19 us -> 3.96 us  [shards(): yp = lax.ppermute(y, 'sector', [(i, i + 1) for i in range(sectors - 1)])]
    dot_general x7 -> x0, matrix products: 14.5 us -> none  [the longest x4 8.35 us: column_product(): lax.dot_general(left, right, (((0,), (0,)), ((), ())), preferred_element_...]
    unnamed x16 -> x9, local copies, waits for them, and re-layouts: 10.7 us -> 4.38 us
    ppermute x3 -> x1, starting transfers between devices: 10.1 us -> 4.93 us  [shards(): yp = lax.ppermute(y, 'sector', [(i, i + 1) for i in range(sectors - 1)])]
    another operation x11 -> x0, local copies, waits for them, and re-layouts: 4.07 us -> none
  transfers between devices with their start and end apart: 5 -> 1, of which waited for: 4 -> 1; matrix products, arithmetic and copies ran while one was open for 3% -> 0% of each run, Pallas kernels for 0% -> 13%
where the time goes in v1:
time: 89.9 us; the launch traced here: 88.5 us
  Pallas kernels  74.6 us (83%)
  starting transfers between devices  4.93 us (5%)
  local copies, waits for them, and re-layouts  4.38 us (5%)
  waiting for transfers between devices  3.96 us (4%)
    pallas_call x1, Pallas kernels, front(): pl.pallas_call(lambda *refs: front_kernel(count, *refs), out_shape=(jax.S...  34.8 us
    pallas_call x1, Pallas kernels, tail(): pl.pallas_call(lambda *refs: tail_kernel(count, sectors, *refs), out_shap...  28.4 us
    pallas_call x1, Pallas kernels, factor(): pl.pallas_call(factor_kernel, out_shape=jax.ShapeDtypeStruct((N, LANES),...  11.5 us
    ppermute x1, starting transfers between devices, shards(): yp = lax.ppermute(y, 'sector', [(i, i + 1) for i in range(sectors - 1)])  4.93 us
    unnamed x9, local copies, waits for them, and re-layouts  4.38 us
    ppermute x1, waiting for transfers between devices, shards(): yp = lax.ppermute(y, 'sector', [(i, i + 1) for i in range(sectors - 1)])  3.96 us
  transfers between devices with their start and end apart: 1, of which 1 were waited for; matrix products, arithmetic and copies ran while one was open for 0% of the time, Pallas kernels for 13%

profile of v1, /device:TPU:97, one launch (start us, length us, event | category | flops | bytes accessed | tf_op | source)
XLA Modules:
  0.0 88.5 jit_solution(13822579874989258572)
XLA Ops:
  0.6 34.8 %front.1 = (bf16[300,1280]{1,0:T(8,128)(2,1)}, f32[3,304,128]{2,1,0:T(8,128)}) custom-call(s32[10,2,10]{2,1,0:T(2,128)} %bitcast.20, bf16[300,1280]{1,0:T(8,128)(2,1)} %bitcast.13, bf16[1280,1280]{1,0:T(8,128)(2,1)} %bitcast.18, bf16[1280,1280]{1,0:T(8,128)(2,1)} %bitcast.19), custom_call_target="tpu_custom_call" | custom-call | tf_op jit(solution)/shard_map/front/pallas_call | solution.py:302
  35.4 4.9 %collective-permute-start = (bf16[300,1280]{1,0:T(8,128)(2,1)}, bf16[300,1280]{1,0:T(8,128)(2,1)S(1)}, u32[]{:S(2)}, u32[]{:S(2)}) collective-permute-start(bf16[300,1280]{1,0:T(8,128)(2,1)} %get-tuple-element.8.refs_1_), channel_id=1, source_target_pairs={{0,32},{32,64},{64,96},{96,128},{128,160},{160,192},{192,224},{1,3... | collective-permute-start | bytes 2304008 | tf_op jit(solution)/shard_map/ppermute | solution.py:450
  40.3 0.0 copy-start.2
  40.4 1.0 %copy-done.2 = f32[3,304,128]{2,1,0:T(8,128)S(1)} copy-done((f32[3,304,128]{2,1,0:T(8,128)S(1)}, f32[3,304,128]{2,1,0:T(8,128)}, u32[]{:S(2)}) %copy-start.2) | copy-done | bytes 466968
  41.4 0.0 copy-start
  41.4 0.0 copy-start.1
  41.4 11.5 %factor.1.refs_3_ = f32[304,384]{1,0:T(8,128)S(1)} custom-call(f32[3,304,128]{2,1,0:T(8,128)S(1)} %copy-done.2), custom_call_target="tpu_custom_call" | custom-call | flops 10000000000 | bytes 1000000 | tf_op jit(solution)/shard_map/factor/pallas_call | solution.py:331
  52.8 4.0 %collective-permute-done.refs_2_ = bf16[300,1280]{1,0:T(8,128)(2,1)S(1)} collective-permute-done((bf16[300,1280]{1,0:T(8,128)(2,1)}, bf16[300,1280]{1,0:T(8,128)(2,1)S(1)}, u32[]{:S(2)}, u32[]{:S(2)}) %collective-permute-start) | collective-permute-done | bytes 768032 | tf_op jit(solution)/shard_map/ppermute | solution.py:450
  56.8 0.0 copy-done
  56.8 0.0 copy-done.1
  56.8 28.4 %tail.1 = (bf16[300,1280]{1,0:T(8,128)(2,1)S(1)}, f32[300,300]{1,0:T(8,128)S(1)}, f32[300,300]{1,0:T(8,128)S(1)}) custom-call(bf16[300,1280]{1,0:T(8,128)(2,1)S(1)} %bitcast.14, bf16[300,1280]{1,0:T(8,128)(2,1)S(1)} %copy-done.1, bf16[300,1280]{1,0:T(8,128)(2,1)S(1)} %collective-permute-done.refs_2_, f32[304,384]{1,0:T(8,128)S(1)} %factor.1.refs_3_), custom_call_target="tpu_custom_call" | custom-call | tf_op jit(solution)/shard_map/tail/pallas_call | solution.py:430
  85.2 1.2 %copy.7 = f32[1,300,300]{2,0,1:T(1,128)} copy(f32[1,300,300]{2,1,0:T(8,128)S(1)} %bitcast.17) | data formatting | bytes 720000
  86.4 1.2 %copy.8 = f32[1,300,300]{2,0,1:T(1,128)} copy(f32[1,300,300]{2,1,0:T(8,128)S(1)} %bitcast.16) | data formatting | bytes 720000
  87.7 0.9 copy.10
Async XLA Ops:
  35.4 21.4 %collective-permute-start = (bf16[300,1280]{1,0:T(8,128)(2,1)}, bf16[300,1280]{1,0:T(8,128)(2,1)S(1)}, u32[]{:S(2)}, u32[]{:S(2)}) collective-permute-start(bf16[300,1280]{1,0:T(8,128)(2,1)} %get-tuple-element.8.refs_1_), channel_id=1, source_target_pairs={{0,32},{32,64},{64,96},{96,128},{128,160},{160,192},{192,224},{1,3... | collective-permute-start | bytes 2304008 | tf_op jit(solution)/shard_map/ppermute | solution.py:450
  40.3 1.0 %copy-start.2 = (f32[3,304,128]{2,1,0:T(8,128)S(1)}, f32[3,304,128]{2,1,0:T(8,128)}, u32[]{:S(2)}) copy-start(f32[3,304,128]{2,1,0:T(8,128)} %get-tuple-element.9.s_ref) | copy-start | bytes 1400836
  41.4 15.4 %copy-start = (bf16[1,1280,300]{1,2,0:T(8,128)(2,1)S(1)}, bf16[1,1280,300]{1,2,0:T(8,128)(2,1)}, u32[]{:S(2)}) copy-start(bf16[1,1280,300]{1,2,0:T(8,128)(2,1)} %param.4) | copy-start | bytes 2304004
  41.4 15.4 %copy-start.1 = (bf16[300,1280]{1,0:T(8,128)(2,1)S(1)}, bf16[300,1280]{1,0:T(8,128)(2,1)}, u32[]{:S(2)}) copy-start(bf16[300,1280]{1,0:T(8,128)(2,1)} %get-tuple-element.8.refs_1_) | copy-start | bytes 2304004

commit v2 on v0

v2 whole, which is shorter than its diff:
```python
import jax
import jax.numpy as jnp
from jax import lax
from jax.experimental import pallas as pl
from jax.experimental.pallas import tpu as pltpu
from jax.sharding import PartitionSpec as P

HI = lax.Precision.HIGHEST
MESH = pl.DeviceIdType.MESH
F32 = jnp.float32
BF16 = jnp.bfloat16
N = 304
LANES = 384
C = 300
ROWS = 1280
CHUNK = 256
NCH = ROWS // CHUNK
BLOCK = 128


def nt(a, b, precision=None):
    return lax.dot_general(a, b, (((1,), (1,)), ((), ())), precision=precision, preferred_element_type=F32)


def tn(a, b, precision=None):
    return lax.dot_general(a, b, (((0,), (0,)), ((), ())), precision=precision, preferred_element_type=F32)


def nn(a, b, precision=None):
    return lax.dot_general(a, b, (((1,), (0,)), ((), ())), precision=precision, preferred_element_type=F32)


def panel_block(tiles, base_lane, count):
    lane = lax.broadcasted_iota(jnp.int32, (8, 128), 1)
    sub = lax.broadcasted_iota(jnp.int32, (8, 128), 0)
    ntile = len(tiles[0])
    for k in range(count):
        lo = 8 * k
        inside = (lane >= lo) & (lane < lo + 8)
        P = tiles[k]
        rows = [[jnp.broadcast_to(P[t][q:q + 1, :], (8, 128)) for t in range(ntile)] for q in range(8)]
        s = [[jnp.broadcast_to(rows[q][0][:, lo + p:lo + p + 1], (8, 128)) if p >= q else None for p in range(8)] for q in range(8)]
        for q in range(8):
            rows[q][0] = jnp.where(inside, jnp.where(lane == lo + q, 1.0, 0.0), rows[q][0])
        u = [[None] * 8 for _ in range(8)]
        rs = [None] * 8
        for p in range(8):
            rs[p] = lax.rsqrt(s[p][p])
            for r in range(p + 1, 8):
                u[p][r] = s[p][r] * rs[p]
            for q in range(p + 1, 8):
                for r in range(q, 8):
                    s[q][r] = s[q][r] - u[p][q] * u[p][r]
            rows[p] = [x * rs[p] for x in rows[p]]
            for q in range(p + 1, 8):
                rows[q] = [x - u[p][q] * y for x, y in zip(rows[q], rows[p])]
        fin = []
        for t in range(ntile):
            acc = rows[0][t]
            for q in range(1, 8):
                acc = jnp.where(sub == q, rows[q][t], acc)
            fin.append(acc)
        tiles[k] = fin
        for g in range(k + 1, count):
            cols = []
            for p in range(8):
                c = jnp.broadcast_to(tiles[g][0][:, lo + p:lo + p + 1], (8, 128))
                for q in range(p):
                    c = c - cols[q] * u[q][p]
                cols.append(c * rs[p])
            new = list(tiles[g])
            new[0] = jnp.where(inside, 0.0, new[0])
            for t in range(ntile):
                acc = new[t]
                for p in range(8):
                    acc = acc - cols[p] * rows[p][t]
                new[t] = acc
            tiles[g] = new
    return tiles


def iota(shape, dim):
    return lax.broadcasted_iota(jnp.int32, shape, dim)


def pack_symmetric(full, out):
    corner = pltpu.roll(full[256:304, 256:384], 0, 1)
    out[0:80, :] = full[0:80, 0:128]
    low = full[80:128, 0:128]
    out[80:128, :] = jnp.where(iota((48, 128), 1) < 48, corner, low)
    out[128:256, :] = full[0:128, 128:256]
    out[256:384, :] = full[128:256, 128:256]
    out[384:512, :] = full[0:128, 256:384] + pltpu.roll(full[128:256, 256:384], 64, 1)


def unpack_upper(packed):
    top = packed[0:128, :]
    upper = iota((128, 128), 1) >= iota((128, 128), 0)
    b00 = jnp.where(upper, top, top.T)
    b22 = jnp.where(iota((48, 128), 1) < 44, top[80:128, :], 0.0)
    both = packed[384:512, :]
    left = iota((128, 128), 1) < 64
    b02 = jnp.where(left, both, 0.0)
    b12 = jnp.where(left, pltpu.roll(both, 64, 1), 0.0)
    return b00, packed[128:256, :], packed[256:384, :], b02, b12, b22


def split(value):
    high = value.astype(BF16)
    return high, (value - high.astype(F32)).astype(BF16)


def factor_block(w, b, count):
    r0 = BLOCK * b
    order = [b] + [t for t in range(3) if t != b]
    tiles = [[w[t, r0 + 8 * g:r0 + 8 * g + 8, :] for t in order] for g in range(count)]
    tiles = panel_block(tiles, r0, count)
    for g in range(count):
        for i, t in enumerate(order):
            w[t, r0 + 8 * g:r0 + 8 * g + 8, :] = tiles[g][i]


def later_rows(w, b):
    r0, r1 = BLOCK * b, BLOCK * (b + 1)
    left = jnp.concatenate([w[t, r0:r1, :] for t in range(b + 1, 3)], axis=1)
    for t in range(3):
        right = w[t, r0:r1, :]
        if t == b:
            right = jnp.where(iota((BLOCK, BLOCK), 1) <= iota((BLOCK, BLOCK), 0), right, 0.0)
        update = tn(left, right, HI)[:N - r1]
        w[t, r1:N, :] = -update if t == b else w[t, r1:N, :] - update


class Sum:
    def __init__(self, me, sector, count, part, recv, total, sems, scale):
        self.me, self.sector, self.count = me, sector, count
        self.part, self.recv, self.total, self.sems, self.scale = part, recv, total, sems, scale
        self.size = part.shape[0] // count

    def rows_of(self, index):
        return pl.ds(pl.multiple_of(index * self.size, 8), self.size)

    def first(self, k):
        peer = lax.rem(self.me + k, self.count)
        return pltpu.make_async_remote_copy(
            src_ref=self.part.at[self.rows_of(peer)], dst_ref=self.recv.at[k],
            send_sem=self.sems[0].at[k], recv_sem=self.sems[1].at[k],
            device_id=(self.sector, peer), device_id_type=MESH)

    def second(self, k):
        peer = lax.rem(self.me + k, self.count)
        mine = self.total.at[self.rows_of(self.me)]
        return pltpu.make_async_remote_copy(
            src_ref=mine, dst_ref=mine, send_sem=self.sems[2].at[k], recv_sem=self.sems[3].at[k],
            device_id=(self.sector, peer), device_id_type=MESH)

    def each(self, action):
        def body(k, carry):
            action(k)
            return carry

        lax.fori_loop(1, self.count, body, 0)

    def scatter(self):
        self.each(lambda k: self.first(k).start())

    def gather(self):
        def add(k, acc):
            self.first(k).wait_recv()
            return acc + self.recv[k]

        acc = lax.fori_loop(1, self.count, add, self.part[self.rows_of(self.me), :])
        self.total[self.rows_of(self.me), :] = acc * self.scale
        self.each(lambda k: self.second(k).start())

    def finish(self):
        self.each(lambda k: self.second(k).wait_recv())

    def drain(self):
        def body(k):
            self.first(k).wait_send()
            self.second(k).wait_send()

        self.each(body)


SYM = 512
CROSS = 768
SPANS = ((0, 0, 128), (1, 128, 256), (2, 256, 304))


def kernel(count, sectors, pattern, x_hbm, d_hbm, r_hbm, q_out, h_out, c_out,
           xv, xn, dv, rv, acc, cs, cr, yv, yp, full, part, recv, total, part2, recv2, total2, w, linv, linvp,
           load, xsend, xrecv, csend, crecv, zsend, zrecv, lsend, lrecv, a1, a2, a3, a4, b1, b2, b3, b4):
    me = lax.axis_index("rows")
    sector = lax.axis_index("sector")
    has_next, has_last = me < count - 1, me > 0
    has_up, has_down = sector < sectors - 1, sector > 0
    columns = [slice(c * CHUNK, (c + 1) * CHUNK) for c in range(NCH)]

    loads = [pltpu.make_async_copy(x_hbm, xv, load.at[0])]
    for i, (source, target) in enumerate(((r_hbm, rv), (d_hbm, dv))):
        for c in range(NCH):
            cols = pl.ds(c * CHUNK, CHUNK)
            loads.append(pltpu.make_async_copy(source.at[:, cols], target.at[:, cols], load.at[1 + i * NCH + c]))
    for l in loads:
        l.start()
    linvp[...] = jnp.zeros((N, LANES), F32)

    barrier = pltpu.get_barrier_semaphore()

    def signal(k, carry):
        pl.semaphore_signal(barrier, inc=1, device_id=(sector, lax.rem(me + k, count)), device_id_type=MESH)
        return carry

    lax.fori_loop(1, count, signal, 0)

    @pl.when(has_down)
    def _():
        pl.semaphore_signal(barrier, inc=1, device_id=(sector - 1, me), device_id_type=MESH)

    @pl.when(has_up)
    def _():
        pl.semaphore_signal(barrier, inc=1, device_id=(sector + 1, me), device_id_type=MESH)

    both = jnp.where(has_down & has_up, 2, 1)
    pl.semaphore_wait(barrier, count - 1 + both)

    def remote(source, target, send, arrive, c, device):
        cols = pl.ds(c * CHUNK, CHUNK)
        return pltpu.make_async_remote_copy(
            src_ref=source.at[:, cols], dst_ref=target.at[:, cols], send_sem=send.at[c], recv_sem=arrive.at[c],
            device_id=device, device_id_type=MESH)

    def x_copy(c):
        return remote(x_hbm, xn, xsend, xrecv, c, (sector, me - 1))

    def c_copy(c):
        return remote(cs, cr, csend, crecv, c, (sector, me + 1))

    def z_copy(c):
        return remote(yv, yp, zsend, zrecv, c, (sector + 1, me))

    def l_copy(b, start, stop):
        piece = (pl.ds(start, stop - start), pl.ds(0, BLOCK * (b + 1)))
        return pltpu.make_async_remote_copy(
            src_ref=linv.at[piece], dst_ref=linvp.at[piece], send_sem=lsend.at[b], recv_sem=lrecv.at[b],
            device_id=(sector + 1, me), device_id_type=MESH)

    @pl.when(has_last)
    def _():
        for c in range(NCH):
            x_copy(c).start()

    full[...] = jnp.zeros((N, LANES), F32)

    @pl.when(sector == 0)
    def _():
        yp[...] = jnp.zeros((C, ROWS), BF16)

    def mask(tile, which, c):
        for i in range(ROWS // BLOCK):
            for j in range(CHUNK // BLOCK):
                row = slice(i * BLOCK, (i + 1) * BLOCK)
                col = slice(c * CHUNK + j * BLOCK, c * CHUNK + (j + 1) * BLOCK)
                keep = pattern[i, which, c * (CHUNK // BLOCK) + j]
                scale = jnp.full((BLOCK, BLOCK), keep.astype(F32)).astype(BF16)
                tile[row, col] = tile[row, col] * scale

    loads[0].wait()
    for c, cols in enumerate(columns):
        loads[1 + c].wait()
        mask(rv, 1, c)
        cs[:, cols] = nn(xv[...], rv[:, cols]).astype(BF16)

        @pl.when(has_next)
        def _():
            c_copy(c).start()

    for c, cols in enumerate(columns):
        loads[1 + NCH + c].wait()
        mask(dv, 0, c)
        acc[:, cols] = nn(xv[...], dv[:, cols])

    for c, cols in enumerate(columns):
        @pl.when(has_next)
        def _():
            x_copy(c).wait_recv()
            for out in columns:
                acc[:, out] += nt(xn[:, cols], rv[out, cols])

    gram = None
    for c, cols in enumerate(columns):
        @pl.when(has_last)
        def _():
            c_copy(c).wait_recv()
            acc[:, cols] += cr[:, cols].astype(F32)

        y = acc[:, cols].astype(BF16)
        yv[:, cols] = y

        @pl.when(has_up)
        def _():
            z_copy(c).start()

        g = nt(y, y)
        gram = g if gram is None else gram + g

    scale = 1.0 / (count * ROWS)
    full[0:C, 0:C] = gram
    pack_symmetric(full, part)
    gram_sum = Sum(me, sector, count, part, recv, total, (a1, a2, a3, a4), scale)
    gram_sum.scatter()
    full[0:C, 0:C] = nt(xv[...], yv[...])
    pack_symmetric(full, part2)
    gram_sum.gather()

    cross = None
    for c, cols in enumerate(columns):
        @pl.when(has_down)
        def _():
            z_copy(c).wait_recv()

        g = nt(yp[:, cols], yv[:, cols])
        cross = g if cross is None else cross + g
    full[0:C, 0:C] = cross
    part2[SYM:SYM + N, :] = full[:, 0:128]
    part2[SYM + N:SYM + 2 * N, :] = full[:, 128:256]
    part2[SYM + 2 * N:SYM + 2 * N + 152, :] = full[0:152, 256:384] + pltpu.roll(full[152:304, 256:384], 64, 1)
    part2[SYM + 2 * N + 152:SYM + CROSS, :] = jnp.zeros((8, BLOCK), F32)
    other_sum = Sum(me, sector, count, part2, recv2, total2, (b1, b2, b3, b4), scale)
    other_sum.scatter()

    gram_sum.finish()
    b00, b01, b11, b02, b12, b22 = unpack_upper(total)
    w[...] = jnp.zeros((3, N, BLOCK), F32)
    w[0, 0:128, :] = b00
    w[1, 0:128, :] = b01
    w[2, 0:128, :] = b02
    w[1, 128:256, :] = b11
    w[2, 128:256, :] = b12
    extra = (iota((48, 128), 0) == iota((48, 128), 1)) & (iota((48, 128), 0) >= 44)
    w[2, 256:304, :] = jnp.where(extra, 1.0, b22)

    for b, start, stop in SPANS:
        factor_block(w, b, (stop - start) // 8)
        if b < 2:
            later_rows(w, b)
        for t in range(3):
            shape = (stop - start, BLOCK)
            keep = iota(shape, 1) + BLOCK * t <= iota(shape, 0) + start
            linv[start:stop, BLOCK * t:BLOCK * (t + 1)] = jnp.where(keep, w[t, start:stop, :], 0.0)

        @pl.when(has_up)
        def _():
            l_copy(b, start, stop).start()

        if b == 0:
            other_sum.gather()

    high, low = split(linv[...])
    for cols in columns:
        block = yv[:, cols]
        q_out[:, cols] = (nn(high[0:C, 0:C], block) + nn(low[0:C, 0:C], block)).astype(BF16)

    other_sum.finish()
    b00, b01, b11, b02, b12, b22 = unpack_upper(total2)
    h_out[0:128, 0:128] = b00
    h_out[0:128, 128:256] = b01
    h_out[0:128, 256:C] = b02[:, 0:44]
    h_out[128:256, 0:128] = b01.T
    h_out[128:256, 128:256] = b11
    h_out[128:256, 256:C] = b12[:, 0:44]
    h_out[256:C, 0:128] = b02.T[0:44]
    h_out[256:C, 128:256] = b12.T[0:44]
    h_out[256:C, 256:C] = b22[0:44, 0:44]
    full[:, 0:128] = total2[SYM:SYM + N, :]
    full[:, 128:256] = total2[SYM + N:SYM + 2 * N, :]
    last = total2[SYM + 2 * N:SYM + 2 * N + 152, :]
    left = iota((152, BLOCK), 1) < 64
    full[0:152, 256:384] = jnp.where(left, last, 0.0)
    full[152:304, 256:384] = jnp.where(left, pltpu.roll(last, 64, 1), 0.0)
    right = nt(full[...], linv[...], HI)

    @pl.when(has_down)
    def _():
        for span in SPANS:
            l_copy(*span).wait_recv()

    c_out[...] = nn(linvp[:, 0:N], right, HI)[0:C, 0:C]

    for c in range(NCH):
        @pl.when(has_last)
        def _():
            x_copy(c).wait_send()

        @pl.when(has_next)
        def _():
            c_copy(c).wait_send()

        @pl.when(has_up)
        def _():
            z_copy(c).wait_send()

    @pl.when(has_up)
    def _():
        for span in SPANS:
            l_copy(*span).wait_send()

    gram_sum.drain()
    other_sum.drain()


def shards(x_block, h_diag, h_right, pattern):
    count, sectors = lax.axis_size("rows"), lax.axis_size("sector")
    dma = pltpu.SemaphoreType.DMA
    vmem = pl.BlockSpec(memory_space=pltpu.VMEM)
    rows_b, square, size = (C, ROWS), (ROWS, ROWS), SYM + CROSS
    q, h, corr = pl.pallas_call(
        lambda *refs: kernel(count, sectors, *refs),
        out_shape=(jax.ShapeDtypeStruct((C, ROWS), BF16), jax.ShapeDtypeStruct((C, C), F32),
                   jax.ShapeDtypeStruct((C, C), F32)),
        in_specs=[pl.BlockSpec(memory_space=pltpu.SMEM)] + [pl.BlockSpec(memory_space=pl.ANY)] * 3,
        out_specs=(vmem,) * 3,
        scratch_shapes=[
            pltpu.VMEM(rows_b, BF16), pltpu.VMEM(rows_b, BF16), pltpu.VMEM(square, BF16), pltpu.VMEM(square, BF16),
            pltpu.VMEM(rows_b, F32), pltpu.VMEM(rows_b, BF16), pltpu.VMEM(rows_b, BF16), pltpu.VMEM(rows_b, BF16),
            pltpu.VMEM(rows_b, BF16), pltpu.VMEM((N, LANES), F32),
            pltpu.VMEM((SYM, BLOCK), F32), pltpu.VMEM((count, SYM // count, BLOCK), F32), pltpu.VMEM((SYM, BLOCK), F32),
            pltpu.VMEM((size, BLOCK), F32), pltpu.VMEM((count, size // count, BLOCK), F32),
            pltpu.VMEM((size, BLOCK), F32),
            pltpu.VMEM((3, N, BLOCK), F32), pltpu.VMEM((N, LANES), F32), pltpu.VMEM((N, LANES), F32),
            dma((1 + 2 * NCH,)), dma((NCH,)), dma((NCH,)), dma((NCH,)), dma((NCH,)), dma((NCH,)), dma((NCH,)),
            dma((3,)), dma((3,)),
        ] + [dma((count,))] * 8,
        compiler_params=pltpu.CompilerParams(collective_id=0, has_side_effects=True, vmem_limit_bytes=60 << 20),
        name="step",
    )(jnp.swapaxes(pattern[0], 0, 1), x_block[0].T, h_diag[0], h_right[0])
    return q.T[None], h[None], corr[None]


def solution(mesh):
    in_specs = (
        P("sector", "rows", None),
        P("sector", "rows", None),
        P("sector", "rows", None),
        P("sector", None, "rows", None),
    )
    out_specs = (P("sector", "rows", None), P("sector", None, None), P("sector", None, None))
    return jax.shard_map(shards, mesh=mesh, in_specs=in_specs, out_specs=out_specs, check_vma=False)
```

time: 393 us -> 67.7 us (0.17)
  the two profiles are of different devices: /device:TPU:97 before, /device:TPU:201 now
where the time goes in v2:
time: 67.7 us; the launch traced here: 67.4 us
  Pallas kernels  60.2 us (89%)
  local copies, waits for them, and re-layouts  6.58 us (10%)
    pallas_call x1, Pallas kernels, shards(): pl.pallas_call(lambda *refs: kernel(count, sectors, *refs), out_shape=(ja...  60.2 us
    unnamed x3, local copies, waits for them, and re-layouts  6.58 us

profile of v2, /device:TPU:201, one launch (start us, length us, event | category | flops | bytes accessed | tf_op | source)
XLA Modules:
  0.0 67.4 jit_solution(9836690201650408653)
XLA Ops:
  0.6 60.2 %step.1 = (bf16[300,1280]{1,0:T(8,128)(2,1)}, f32[300,300]{1,0:T(8,128)}, f32[300,300]{1,0:T(8,128)}) custom-call(s32[10,2,10]{2,1,0:T(2,128)} %bitcast.19, bf16[300,1280]{1,0:T(8,128)(2,1)} %bitcast.16, bf16[1280,1280]{1,0:T(8,128)(2,1)} %bitcast.13, bf16[1280,1280]{1,0:T(8,128)(2,1)} %bitcast.14), custom_call_target="tpu_custom_call" | custom-call | tf_op jit(solution)/shard_map/step/pallas_call | solution.py:419
  60.9 2.3 %copy.7 = f32[1,300,300]{2,0,1:T(1,128)} copy(f32[1,300,300]{2,1,0:T(8,128)} %bitcast.18) | data formatting | bytes 720000
  63.1 2.3 %copy.8 = f32[1,300,300]{2,0,1:T(1,128)} copy(f32[1,300,300]{2,1,0:T(8,128)} %bitcast.17) | data formatting | bytes 720000
  65.4 2.1 %copy.10 = bf16[1,1280,300]{1,2,0:T(8,128)(2,1)} copy(bf16[1,1280,300]{1,2,0:T(8,128)(2,1)} %bitcast.15) | data formatting | bytes 1536000

commit v3 on v2

--- a/solution.py
+++ b/solution.py
@@ -189,13 +189,16 @@
 SPANS = ((0, 0, 128), (1, 128, 256), (2, 256, 304))
 
 
-def kernel(count, sectors, pattern, x_hbm, d_hbm, r_hbm, q_out, h_out, c_out,
-           xv, xn, dv, rv, acc, cs, cr, yv, yp, full, part, recv, total, part2, recv2, total2, w, linv, linvp,
-           load, xsend, xrecv, csend, crecv, zsend, zrecv, lsend, lrecv, a1, a2, a3, a4, b1, b2, b3, b4):
+def kernel(count, sectors, pattern, x_hbm, d_hbm, r_hbm, q_out, sums_out, linv_out, linvp_out,
+           xv, xn, dv, rv, acc, cs, cr, yv, yp, full, part, recv, total, part_h, recv_h, part_c, recv_c, total2, w, linv, linvp, qv,
+           load, xsend, xrecv, csend, crecv, zsend, zrecv, lsend, lrecv, outsem, a1, a2, a3, a4, h1, h2, c1, c2, b1, b2):
     me = lax.axis_index("rows")
     sector = lax.axis_index("sector")
     has_next, has_last = me < count - 1, me > 0
     has_up, has_down = sector < sectors - 1, sector > 0
+    core = lax.rem(me, 2)
+    z_sends = ((core == 0) & has_up) | ((core == 1) & has_down)
+    z_arrives = ((core == 0) & has_down) | ((core == 1) & has_up)
     columns = [slice(c * CHUNK, (c + 1) * CHUNK) for c in range(NCH)]
 
     loads = [pltpu.make_async_copy(x_hbm, xv, load.at[0])]
@@ -217,14 +220,23 @@
 
     @pl.when(has_down)
     def _():
+        def signal_below(k, carry):
+            pl.semaphore_signal(barrier, inc=1, device_id=(sector - 1, 2 * k + 1), device_id_type=MESH)
+            return carry
+
+        lax.fori_loop(0, count // 2, signal_below, 0)
+
+    @pl.when(has_down & (core == 0))
+    def _():
         pl.semaphore_signal(barrier, inc=1, device_id=(sector - 1, me), device_id_type=MESH)
 
-    @pl.when(has_up)
+    @pl.when(has_up & (core == 1))
     def _():
         pl.semaphore_signal(barrier, inc=1, device_id=(sector + 1, me), device_id_type=MESH)
 
-    both = jnp.where(has_down & has_up, 2, 1)
-    pl.semaphore_wait(barrier, count - 1 + both)
+    above = jnp.where(has_up, jnp.where(core == 1, count, 1), 0)
+    below = jnp.where(has_down & (core == 1), 1, 0)
+    pl.semaphore_wait(barrier, count - 1 + above + below)
 
     def remote(source, target, send, arrive, c, device):
         cols = pl.ds(c * CHUNK, CHUNK)
@@ -239,7 +251,7 @@
         return remote(cs, cr, csend, crecv, c, (sector, me + 1))
 
     def z_copy(c):
-        return remote(yv, yp, zsend, zrecv, c, (sector + 1, me))
+        return remote(yv, yp, zsend, zrecv, c, (sector + 1 - 2 * core, me))
 
     def l_copy(b, start, stop):
         piece = (pl.ds(start, stop - start), pl.ds(0, BLOCK * (b + 1)))
@@ -253,10 +265,6 @@
             x_copy(c).start()
 
     full[...] = jnp.zeros((N, LANES), F32)
-
-    @pl.when(sector == 0)
-    def _():
-        yp[...] = jnp.zeros((C, ROWS), BF16)
 
     def mask(tile, which, c):
         for i in range(ROWS // BLOCK):
@@ -299,7 +307,7 @@
         y = acc[:, cols].astype(BF16)
         yv[:, cols] = y
 
-        @pl.when(has_up)
+        @pl.when(z_sends)
         def _():
             z_copy(c).start()
 
@@ -312,24 +320,81 @@
     gram_sum = Sum(me, sector, count, part, recv, total, (a1, a2, a3, a4), scale)
     gram_sum.scatter()
     full[0:C, 0:C] = nt(xv[...], yv[...])
-    pack_symmetric(full, part2)
+    pack_symmetric(full, part_h)
     gram_sum.gather()
 
-    cross = None
+    def each(lower, action):
+        def body(k, carry):
+            action(k)
+            return carry
+
+        lax.fori_loop(lower, count, body, 0)
+
+    size_h, size_c = SYM // count, CROSS // count
+
+    def chunk(index, size):
+        return pl.ds(pl.multiple_of(index * size, 8), size)
+
+    def h_copy(k):
+        peer = lax.rem(me + k, count)
+        return pltpu.make_async_remote_copy(
+            src_ref=part_h.at[chunk(peer, size_h)], dst_ref=recv_h.at[k], send_sem=h1.at[k], recv_sem=h2.at[k],
+            device_id=(sector, peer), device_id_type=MESH)
+
+    def cross_copy(k):
+        peer = lax.rem(me + k, count)
+        return pltpu.make_async_remote_copy(
+            src_ref=part_c.at[chunk(peer, size_c)], dst_ref=recv_c.at[k], send_sem=c1.at[k], recv_sem=c2.at[k],
+            device_id=(sector + core, peer), device_id_type=MESH)
+
+    def all_copy(k):
+        peer = lax.rem(me + k, count)
+        return pltpu.make_async_remote_copy(
+            src_ref=total2.at[me], dst_ref=total2.at[me], send_sem=b1.at[k], recv_sem=b2.at[k],
+            device_id=(sector, peer), device_id_type=MESH)
+
+    each(1, lambda k: h_copy(k).start())
+    full[...] = jnp.zeros((N, LANES), F32)
     for c, cols in enumerate(columns):
+        @pl.when(z_arrives)
+        def _():
+            z_copy(c).wait_recv()
+
+        @pl.when(z_arrives & (core == 0))
+        def _():
+            full[0:C, 0:C] += nt(yp[:, cols], yv[:, cols])
+
+        @pl.when(z_arrives & (core == 1))
+        def _():
+            full[0:C, 0:C] += nt(yv[:, cols], yp[:, cols])
+
+    part_c[0:N, :] = full[:, 0:128]
+    part_c[N:2 * N, :] = full[:, 128:256]
+    part_c[2 * N:2 * N + 152, :] = full[0:152, 256:384] + pltpu.roll(full[152:304, 256:384], 64, 1)
+    part_c[2 * N + 152:CROSS, :] = jnp.zeros((8, BLOCK), F32)
+
+    @pl.when(z_arrives)
+    def _():
+        each(1 - core, lambda k: cross_copy(k).start())
+
+    def gather_both():
+        def add_h(k, value):
+            h_copy(k).wait_recv()
+            return value + recv_h[k]
+
+        def add_c(k, value):
+            cross_copy(k).wait_recv()
+            return value + recv_c[k]
+
+        total2[me, 0:size_h, :] = lax.fori_loop(1, count, add_h, part_h[chunk(me, size_h), :]) * scale
+        total2[me, size_h:size_h + size_c, :] = jnp.zeros((size_c, BLOCK), F32)
+
         @pl.when(has_down)
         def _():
-            z_copy(c).wait_recv()
-
-        g = nt(yp[:, cols], yv[:, cols])
-        cross = g if cross is None else cross + g
-    full[0:C, 0:C] = cross
-    part2[SYM:SYM + N, :] = full[:, 0:128]
-    part2[SYM + N:SYM + 2 * N, :] = full[:, 128:256]
-    part2[SYM + 2 * N:SYM + 2 * N + 152, :] = full[0:152, 256:384] + pltpu.roll(full[152:304, 256:384], 64, 1)
-    part2[SYM + 2 * N + 152:SYM + CROSS, :] = jnp.zeros((8, BLOCK), F32)
-    other_sum = Sum(me, sector, count, part2, recv2, total2, (b1, b2, b3, b4), scale)
-    other_sum.scatter()
+            own = jnp.where(core == 0, part_c[chunk(me, size_c), :], 0.0)
+            total2[me, size_h:size_h + size_c, :] = lax.fori_loop(1 - core, count, add_c, own) * scale
+
+        each(1, lambda k: all_copy(k).start())
 
     gram_sum.finish()
     b00, b01, b11, b02, b12, b22 = unpack_upper(total)
@@ -356,59 +421,107 @@
             l_copy(b, start, stop).start()
 
         if b == 0:
-            other_sum.gather()
-
+            gather_both()
+
+    outs = [pltpu.make_async_copy(linv, linv_out, outsem.at[NCH])]
+    outs[0].start()
     high, low = split(linv[...])
-    for cols in columns:
+    for c, cols in enumerate(columns):
         block = yv[:, cols]
-        q_out[:, cols] = (nn(high[0:C, 0:C], block) + nn(low[0:C, 0:C], block)).astype(BF16)
-
-    other_sum.finish()
-    b00, b01, b11, b02, b12, b22 = unpack_upper(total2)
-    h_out[0:128, 0:128] = b00
-    h_out[0:128, 128:256] = b01
-    h_out[0:128, 256:C] = b02[:, 0:44]
-    h_out[128:256, 0:128] = b01.T
-    h_out[128:256, 128:256] = b11
-    h_out[128:256, 256:C] = b12[:, 0:44]
-    h_out[256:C, 0:128] = b02.T[0:44]
-    h_out[256:C, 128:256] = b12.T[0:44]
-    h_out[256:C, 256:C] = b22[0:44, 0:44]
-    full[:, 0:128] = total2[SYM:SYM + N, :]
-    full[:, 128:256] = total2[SYM + N:SYM + 2 * N, :]
-    last = total2[SYM + 2 * N:SYM + 2 * N + 152, :]
+        qv[:, cols] = (nn(high[0:C, 0:C], block) + nn(low[0:C, 0:C], block)).astype(BF16)
+        piece = pl.ds(c * CHUNK, CHUNK)
+        outs.append(pltpu.make_async_copy(qv.at[:, piece], q_out.at[:, piece], outsem.at[c]))
+        outs[-1].start()
+
+    @pl.when(has_down)
+    def _():
+        for span in SPANS:
+            l_copy(*span).wait_recv()
+
+    outs.append(pltpu.make_async_copy(linvp, linvp_out, outsem.at[NCH + 1]))
+    outs[-1].start()
+    each(1, lambda k: all_copy(k).wait_recv())
+    outs.append(pltpu.make_async_copy(total2, sums_out, outsem.at[NCH + 2]))
+    outs[-1].start()
+    for copy in outs:
+        copy.wait()
+
+    for c in range(NCH):
+        @pl.when(has_last)
+        def _():
+            x_copy(c).wait_send()
+
+        @pl.when(has_next)
+        def _():
+            c_copy(c).wait_send()
+
+        @pl.when(z_sends)
+        def _():
+            z_copy(c).wait_send()
+
+    @pl.when(has_up)
+    def _():
+        for span in SPANS:
+            l_copy(*span).wait_send()
+
+    gram_sum.drain()
+
+    def drain(k):
+        h_copy(k).wait_send()
+        all_copy(k).wait_send()
+
+    each(1, drain)
+
+    @pl.when(z_arrives)
+    def _():
+        each(1 - core, lambda k: cross_copy(k).wait_send())
+
+
+def finish_kernel(q_in, sums_in, linv_in, linvp_in, q_out, h_out, c_out, sums, linv, linvp, full, q, sem):
+    pairs = ((q_in, q), (sums_in, sums), (linv_in, linv), (linvp_in, linvp))
+    copies = [pltpu.make_async_copy(*pair, sem.at[i]) for i, pair in enumerate(pairs)]
+    for copy in copies:
+        copy.start()
+    copies[0].wait()
+    q_copy = pltpu.make_async_copy(q, q_out, sem.at[4])
+    q_copy.start()
+    for copy in copies[1:]:
+        copy.wait()
+    count, size = sums.shape[0], SYM // sums.shape[0]
+    cross = sums[:, size:, :].reshape(CROSS, BLOCK)
+    full[:, 0:128] = cross[0:N]
+    full[:, 128:256] = cross[N:2 * N]
+    last = cross[2 * N:2 * N + 152]
     left = iota((152, BLOCK), 1) < 64
     full[0:152, 256:384] = jnp.where(left, last, 0.0)
     full[152:304, 256:384] = jnp.where(left, pltpu.roll(last, 64, 1), 0.0)
     right = nt(full[...], linv[...], HI)
-
-    @pl.when(has_down)
-    def _():
-        for span in SPANS:
-            l_copy(*span).wait_recv()
-
-    c_out[...] = nn(linvp[:, 0:N], right, HI)[0:C, 0:C]
-
-    for c in range(NCH):
-        @pl.when(has_last)
-        def _():
-            x_copy(c).wait_send()
-
-        @pl.when(has_next)
-        def _():
-            c_copy(c).wait_send()
-
-        @pl.when(has_up)
-        def _():
-            z_copy(c).wait_send()
-
-    @pl.when(has_up)
-    def _():
-        for span in SPANS:
-            l_copy(*span).wait_send()
-
-    gram_sum.drain()
-    other_sum.drain()
+    c_out[:, 0, :] = nn(linvp[:, 0:N], right, HI)[0:C, 0:C]
+    b00, b01, b11, b02, b12, b22 = unpack_upper(sums[:, 0:size, :].reshape(SYM, BLOCK))
+    full[0:128, 0:128] = b00
+    full[0:128, 128:256] = b01
+    full[0:128, 256:384] = b02
+    full[128:256, 0:128] = b01.T
+    full[128:256, 128:256] = b11
+    full[128:256, 256:384] = b12
+    full[256:304, 0:128] = b02.T[0:48]
+    full[256:304, 128:256] = b12.T[0:48]
+    full[256:304, 256:384] = b22
+    h_out[:, 0, :] = full[0:C, 0:C]
+    q_copy.wait()
+
+
+def finish(q, sums, linv, linvp):
+    vmem = pl.BlockSpec(memory_space=pltpu.VMEM)
+    anywhere = pl.BlockSpec(memory_space=pl.ANY)
+    square = jax.ShapeDtypeStruct((C, 1, C), F32)
+    return pl.pallas_call(
+        finish_kernel, out_shape=(jax.ShapeDtypeStruct((C, ROWS), BF16), square, square),
+        in_specs=[anywhere] * 4, out_specs=(anywhere, vmem, vmem),
+        scratch_shapes=[pltpu.VMEM(sums.shape, F32)] + [pltpu.VMEM((N, LANES), F32)] * 3
+        + [pltpu.VMEM((C, ROWS), BF16), pltpu.SemaphoreType.DMA((5,))],
+        compiler_params=pltpu.CompilerParams(vmem_limit_bytes=57 << 20), name="finish",
+    )(q, sums, linv, linvp)
 
 
 def shards(x_block, h_diag, h_right, pattern):
@@ -416,27 +529,30 @@
     dma = pltpu.SemaphoreType.DMA
     vmem = pl.BlockSpec(memory_space=pltpu.VMEM)
     rows_b, square, size = (C, ROWS), (ROWS, ROWS), SYM + CROSS
-    q, h, corr = pl.pallas_call(
+    q, sums, linv, linvp = pl.pallas_call(
         lambda *refs: kernel(count, sectors, *refs),
-        out_shape=(jax.ShapeDtypeStruct((C, ROWS), BF16), jax.ShapeDtypeStruct((C, C), F32),
-                   jax.ShapeDtypeStruct((C, C), F32)),
+        out_shape=(jax.ShapeDtypeStruct((C, ROWS), BF16), jax.ShapeDtypeStruct((count, size // count, BLOCK), F32),
+                   jax.ShapeDtypeStruct((N, LANES), F32), jax.ShapeDtypeStruct((N, LANES), F32)),
         in_specs=[pl.BlockSpec(memory_space=pltpu.SMEM)] + [pl.BlockSpec(memory_space=pl.ANY)] * 3,
-        out_specs=(vmem,) * 3,
+        out_specs=(pl.BlockSpec(memory_space=pl.ANY),) * 4,
         scratch_shapes=[
             pltpu.VMEM(rows_b, BF16), pltpu.VMEM(rows_b, BF16), pltpu.VMEM(square, BF16), pltpu.VMEM(square, BF16),
             pltpu.VMEM(rows_b, F32), pltpu.VMEM(rows_b, BF16), pltpu.VMEM(rows_b, BF16), pltpu.VMEM(rows_b, BF16),
             pltpu.VMEM(rows_b, BF16), pltpu.VMEM((N, LANES), F32),
             pltpu.VMEM((SYM, BLOCK), F32), pltpu.VMEM((count, SYM // count, BLOCK), F32), pltpu.VMEM((SYM, BLOCK), F32),
-            pltpu.VMEM((size, BLOCK), F32), pltpu.VMEM((count, size // count, BLOCK), F32),
-            pltpu.VMEM((size, BLOCK), F32),
+            pltpu.VMEM((SYM, BLOCK), F32), pltpu.VMEM((count, SYM // count, BLOCK), F32),
+            pltpu.VMEM((CROSS, BLOCK), F32), pltpu.VMEM((count, CROSS // count, BLOCK), F32),
+            pltpu.VMEM((count, size // count, BLOCK), F32),
             pltpu.VMEM((3, N, BLOCK), F32), pltpu.VMEM((N, LANES), F32), pltpu.VMEM((N, LANES), F32),
+            pltpu.VMEM(rows_b, BF16),
             dma((1 + 2 * NCH,)), dma((NCH,)), dma((NCH,)), dma((NCH,)), dma((NCH,)), dma((NCH,)), dma((NCH,)),
-            dma((3,)), dma((3,)),
-        ] + [dma((count,))] * 8,
-        compiler_params=pltpu.CompilerParams(collective_id=0, has_side_effects=True, vmem_limit_bytes=60 << 20),
+            dma((3,)), dma((3,)), dma((NCH + 3,)),
+        ] + [dma((count,))] * 10,
+        compiler_params=pltpu.CompilerParams(collective_id=0, has_side_effects=True, vmem_limit_bytes=57 << 20),
         name="step",
     )(jnp.swapaxes(pattern[0], 0, 1), x_block[0].T, h_diag[0], h_right[0])
-    return q.T[None], h[None], corr[None]
+    q, h, corr = finish(q, sums, linv, linvp)
+    return q.T[None], jnp.swapaxes(h, 0, 1), jnp.swapaxes(corr, 0, 1)
 
 
 def solution(mesh):

time: 67.7 us -> 65.5 us (0.968)
  the two profiles are of different devices: /device:TPU:201 before, /device:TPU:135 now
where the time goes in v3:
time: 65.5 us; the launch traced here: 65.4 us
  Pallas kernels  64.6 us (99%)
  between operations  0.82 us (1%)
    pallas_call x1, Pallas kernels, shards(): pl.pallas_call(lambda *refs: kernel(count, sectors, *refs), out_shape=(ja...  59.7 us
    pallas_call x1, Pallas kernels, finish(): pl.pallas_call(finish_kernel, out_shape=(jax.ShapeDtypeStruct((C, ROWS),...  4.9 us

profile of v3, /device:TPU:135, one launch (start us, length us, event | category | flops | bytes accessed | tf_op | source)
XLA Modules:
  0.0 65.4 jit_solution(15200962764713598432)
XLA Ops:
  0.6 59.7 %step.1 = (bf16[300,1280]{1,0:T(8,128)(2,1)}, f32[32,40,128]{2,1,0:T(8,128)}, f32[304,384]{1,0:T(8,128)}, f32[304,384]{1,0:T(8,128)}) custom-call(s32[10,2,10]{2,1,0:T(2,128)} %bitcast.16, bf16[300,1280]{1,0:T(8,128)(2,1)} %bitcast.15, bf16[1280,1280]{1,0:T(8,128)(2,1)} %bitcast.13, bf16[1280,1280]{1,0:T(8,128)(2,1)} %bitcast.14), custom_call_target="tpu_custom_call" | custom-call | tf_op jit(solution)/shard_map/step/pallas_call | solution.py:532
  60.3 4.9 %finish.1 = (bf16[300,1280]{1,0:T(8,128)(2,1)}, f32[300,1,300]{2,1,0:T(1,128)}, f32[300,1,300]{2,1,0:T(1,128)}) custom-call(bf16[300,1280]{1,0:T(8,128)(2,1)} %get-tuple-element.10.q_in, f32[32,40,128]{2,1,0:T(8,128)} %get-tuple-element.11.sums_in, f32[304,384]{1,0:T(8,128)} %get-tuple-element.12.linv_in, f32[304,384]{1,0:T(8,128)} %get-tuple-element.13.linvp_in), custom_call_target="tpu_custom_call" | custom-call | tf_op jit(solution)/shard_map/finish/pallas_call | solution.py:518

commit v4 on v3

--- a/solution.py
+++ b/solution.py
@@ -131,66 +131,26 @@
         w[t, r1:N, :] = -update if t == b else w[t, r1:N, :] - update
 
 
-class Sum:
-    def __init__(self, me, sector, count, part, recv, total, sems, scale):
-        self.me, self.sector, self.count = me, sector, count
-        self.part, self.recv, self.total, self.sems, self.scale = part, recv, total, sems, scale
-        self.size = part.shape[0] // count
-
-    def rows_of(self, index):
-        return pl.ds(pl.multiple_of(index * self.size, 8), self.size)
-
-    def first(self, k):
-        peer = lax.rem(self.me + k, self.count)
-        return pltpu.make_async_remote_copy(
-            src_ref=self.part.at[self.rows_of(peer)], dst_ref=self.recv.at[k],
-            send_sem=self.sems[0].at[k], recv_sem=self.sems[1].at[k],
-            device_id=(self.sector, peer), device_id_type=MESH)
-
-    def second(self, k):
-        peer = lax.rem(self.me + k, self.count)
-        mine = self.total.at[self.rows_of(self.me)]
-        return pltpu.make_async_remote_copy(
-            src_ref=mine, dst_ref=mine, send_sem=self.sems[2].at[k], recv_sem=self.sems[3].at[k],
-            device_id=(self.sector, peer), device_id_type=MESH)
-
-    def each(self, action):
-        def body(k, carry):
-            action(k)
-            return carry
-
-        lax.fori_loop(1, self.count, body, 0)
-
-    def scatter(self):
-        self.each(lambda k: self.first(k).start())
-
-    def gather(self):
-        def add(k, acc):
-            self.first(k).wait_recv()
-            return acc + self.recv[k]
-
-        acc = lax.fori_loop(1, self.count, add, self.part[self.rows_of(self.me), :])
-        self.total[self.rows_of(self.me), :] = acc * self.scale
-        self.each(lambda k: self.second(k).start())
-
-    def finish(self):
-        self.each(lambda k: self.second(k).wait_recv())
-
-    def drain(self):
-        def body(k):
-            self.first(k).wait_send()
-            self.second(k).wait_send()
-
-        self.each(body)
+def take(view, sem):
+    pltpu.make_async_copy(view, view, sem).wait()
+
+
+def each(lower, upper, action):
+    def body(k, carry):
+        action(k)
+        return carry
+
+    lax.fori_loop(lower, upper, body, 0)
 
 
 SYM = 512
 CROSS = 768
+EARLY = 3
 SPANS = ((0, 0, 128), (1, 128, 256), (2, 256, 304))
 
 
-def kernel(count, sectors, pattern, x_hbm, d_hbm, r_hbm, q_out, sums_out, linv_out, linvp_out,
-           xv, xn, dv, rv, acc, cs, cr, yv, yp, full, part, recv, total, part_h, recv_h, part_c, recv_c, total2, w, linv, linvp, qv,
+def kernel(count, sectors, pattern, x_hbm, d_hbm, r_hbm, q_out, sums_out, right_out, linvp_out,
+           xv, xn, dv, rv, acc, cs, cr, yv, yp, full, part, recv, total, part_h, recv_h, part_c, recv_c, total2, w, linv, linvp, qv, right,
            load, xsend, xrecv, csend, crecv, zsend, zrecv, lsend, lrecv, outsem, a1, a2, a3, a4, h1, h2, c1, c2, b1, b2):
     me = lax.axis_index("rows")
     sector = lax.axis_index("sector")
@@ -236,36 +196,6 @@
 
     above = jnp.where(has_up, jnp.where(core == 1, count, 1), 0)
     below = jnp.where(has_down & (core == 1), 1, 0)
-    pl.semaphore_wait(barrier, count - 1 + above + below)
-
-    def remote(source, target, send, arrive, c, device):
-        cols = pl.ds(c * CHUNK, CHUNK)
-        return pltpu.make_async_remote_copy(
-            src_ref=source.at[:, cols], dst_ref=target.at[:, cols], send_sem=send.at[c], recv_sem=arrive.at[c],
-            device_id=device, device_id_type=MESH)
-
-    def x_copy(c):
-        return remote(x_hbm, xn, xsend, xrecv, c, (sector, me - 1))
-
-    def c_copy(c):
-        return remote(cs, cr, csend, crecv, c, (sector, me + 1))
-
-    def z_copy(c):
-        return remote(yv, yp, zsend, zrecv, c, (sector + 1 - 2 * core, me))
-
-    def l_copy(b, start, stop):
-        piece = (pl.ds(start, stop - start), pl.ds(0, BLOCK * (b + 1)))
-        return pltpu.make_async_remote_copy(
-            src_ref=linv.at[piece], dst_ref=linvp.at[piece], send_sem=lsend.at[b], recv_sem=lrecv.at[b],
-            device_id=(sector + 1, me), device_id_type=MESH)
-
-    @pl.when(has_last)
-    def _():
-        for c in range(NCH):
-            x_copy(c).start()
-
-    full[...] = jnp.zeros((N, LANES), F32)
-
     def mask(tile, which, c):
         for i in range(ROWS // BLOCK):
             for j in range(CHUNK // BLOCK):
@@ -275,11 +205,51 @@
                 scale = jnp.full((BLOCK, BLOCK), keep.astype(F32)).astype(BF16)
                 tile[row, col] = tile[row, col] * scale
 
-    loads[0].wait()
-    for c, cols in enumerate(columns):
+    def remote(source, target, send, arrive, c, device):
+        cols = pl.ds(c * CHUNK, CHUNK)
+        return pltpu.make_async_remote_copy(
+            src_ref=source.at[:, cols], dst_ref=target.at[:, cols], send_sem=send.at[c], recv_sem=arrive.at[c],
+            device_id=device, device_id_type=MESH)
+
+    def x_copy(c):
+        return remote(x_hbm, xn, xsend, xrecv, c, (sector, me - 1))
+
+    def c_copy(c):
+        return remote(cs, cr, csend, crecv, c, (sector, me + 1))
+
+    def z_copy(c):
+        return remote(yv, yp, zsend, zrecv, c, (sector + 1 - 2 * core, me))
+
+    def l_copy(b, start, stop):
+        piece = (pl.ds(start, stop - start), pl.ds(0, BLOCK * (b + 1)))
+        return pltpu.make_async_remote_copy(
+            src_ref=linv.at[piece], dst_ref=linvp.at[piece], send_sem=lsend.at[b], recv_sem=lrecv.at[b],
+            device_id=(sector + 1, me), device_id_type=MESH)
+
+    def carry(c):
+        cols = columns[c]
         loads[1 + c].wait()
         mask(rv, 1, c)
         cs[:, cols] = nn(xv[...], rv[:, cols]).astype(BF16)
+
+    full[...] = jnp.zeros((N, LANES), F32)
+    loads[0].wait()
+    for c in range(EARLY):
+        carry(c)
+    pl.semaphore_wait(barrier, count - 1 + above + below)
+
+    @pl.when(has_last)
+    def _():
+        for c in range(NCH):
+            x_copy(c).start()
+
+    @pl.when(has_next)
+    def _():
+        for c in range(EARLY):
+            c_copy(c).start()
+
+    for c in range(EARLY, NCH):
+        carry(c)
 
         @pl.when(has_next)
         def _():
@@ -317,43 +287,52 @@
     scale = 1.0 / (count * ROWS)
     full[0:C, 0:C] = gram
     pack_symmetric(full, part)
-    gram_sum = Sum(me, sector, count, part, recv, total, (a1, a2, a3, a4), scale)
-    gram_sum.scatter()
+    size_h, size_c = SYM // count, CROSS // count
+
+    def chunk(index, size):
+        return pl.ds(pl.multiple_of(index * size, 8), size)
+
+    def gram_copy(k):
+        peer = lax.rem(me + k, count)
+        return pltpu.make_async_remote_copy(
+            src_ref=part.at[chunk(peer, size_h)], dst_ref=recv.at[k], send_sem=a1, recv_sem=a2,
+            device_id=(sector, peer), device_id_type=MESH)
+
+    def gram_all(k):
+        peer = lax.rem(me + k, count)
+        mine = total.at[chunk(me, size_h)]
+        return pltpu.make_async_remote_copy(
+            src_ref=mine, dst_ref=mine, send_sem=a3, recv_sem=a4, device_id=(sector, peer), device_id_type=MESH)
+
+    others = pl.ds(1, count - 1)
+    each(1, count, lambda k: gram_copy(k).start())
+    recv[0] = part[chunk(me, size_h), :]
     full[0:C, 0:C] = nt(xv[...], yv[...])
     pack_symmetric(full, part_h)
-    gram_sum.gather()
-
-    def each(lower, action):
-        def body(k, carry):
-            action(k)
-            return carry
-
-        lax.fori_loop(lower, count, body, 0)
-
-    size_h, size_c = SYM // count, CROSS // count
-
-    def chunk(index, size):
-        return pl.ds(pl.multiple_of(index * size, 8), size)
+    take(recv.at[others], a2)
+    total[chunk(me, size_h), :] = jnp.sum(recv[...], axis=0) * scale
+    each(1, count, lambda k: gram_all(k).start())
 
     def h_copy(k):
         peer = lax.rem(me + k, count)
         return pltpu.make_async_remote_copy(
-            src_ref=part_h.at[chunk(peer, size_h)], dst_ref=recv_h.at[k], send_sem=h1.at[k], recv_sem=h2.at[k],
+            src_ref=part_h.at[chunk(peer, size_h)], dst_ref=recv_h.at[k], send_sem=h1, recv_sem=h2,
             device_id=(sector, peer), device_id_type=MESH)
 
     def cross_copy(k):
         peer = lax.rem(me + k, count)
         return pltpu.make_async_remote_copy(
-            src_ref=part_c.at[chunk(peer, size_c)], dst_ref=recv_c.at[k], send_sem=c1.at[k], recv_sem=c2.at[k],
+            src_ref=part_c.at[chunk(peer, size_c)], dst_ref=recv_c.at[k], send_sem=c1, recv_sem=c2,
             device_id=(sector + core, peer), device_id_type=MESH)
 
     def all_copy(k):
         peer = lax.rem(me + k, count)
         return pltpu.make_async_remote_copy(
-            src_ref=total2.at[me], dst_ref=total2.at[me], send_sem=b1.at[k], recv_sem=b2.at[k],
+            src_ref=total2.at[me], dst_ref=total2.at[me], send_sem=b1, recv_sem=b2,
             device_id=(sector, peer), device_id_type=MESH)
 
-    each(1, lambda k: h_copy(k).start())
+    each(1, count, lambda k: h_copy(k).start())
+    recv_h[0] = part_h[chunk(me, size_h), :]
     full[...] = jnp.zeros((N, LANES), F32)
     for c, cols in enumerate(columns):
         @pl.when(z_arrives)
@@ -375,28 +354,37 @@
 
     @pl.when(z_arrives)
     def _():
-        each(1 - core, lambda k: cross_copy(k).start())
+        each(1 - core, count, lambda k: cross_copy(k).start())
+
+    @pl.when(core == 0)
+    def _():
+        recv_c[0] = part_c[chunk(me, size_c), :]
+
+    def take_cross(sem):
+        @pl.when(core == 0)
+        def _():
+            take(recv_c.at[others], sem)
+
+        @pl.when(core == 1)
+        def _():
+            take(recv_c, sem)
 
     def gather_both():
-        def add_h(k, value):
-            h_copy(k).wait_recv()
-            return value + recv_h[k]
-
-        def add_c(k, value):
-            cross_copy(k).wait_recv()
-            return value + recv_c[k]
-
-        total2[me, 0:size_h, :] = lax.fori_loop(1, count, add_h, part_h[chunk(me, size_h), :]) * scale
-        total2[me, size_h:size_h + size_c, :] = jnp.zeros((size_c, BLOCK), F32)
+        take(recv_h.at[others], h2)
+        total2[me, 0:size_h, :] = jnp.sum(recv_h[...], axis=0) * scale
 
         @pl.when(has_down)
         def _():
-            own = jnp.where(core == 0, part_c[chunk(me, size_c), :], 0.0)
-            total2[me, size_h:size_h + size_c, :] = lax.fori_loop(1 - core, count, add_c, own) * scale
-
-        each(1, lambda k: all_copy(k).start())
-
-    gram_sum.finish()
+            take_cross(c2)
+            total2[me, size_h:size_h + size_c, :] = jnp.sum(recv_c[...], axis=0) * scale
+
+        @pl.when(sector == 0)
+        def _():
+            total2[me, size_h:size_h + size_c, :] = jnp.zeros((size_c, BLOCK), F32)
+
+        each(1, count, lambda k: all_copy(k).start())
+
+    take(recv.at[others], a4)
     b00, b01, b11, b02, b12, b22 = unpack_upper(total)
     w[...] = jnp.zeros((3, N, BLOCK), F32)
     w[0, 0:128, :] = b00
@@ -423,8 +411,7 @@
         if b == 0:
             gather_both()
 
-    outs = [pltpu.make_async_copy(linv, linv_out, outsem.at[NCH])]
-    outs[0].start()
+    outs = []
     high, low = split(linv[...])
     for c, cols in enumerate(columns):
         block = yv[:, cols]
@@ -433,15 +420,27 @@
         outs.append(pltpu.make_async_copy(qv.at[:, piece], q_out.at[:, piece], outsem.at[c]))
         outs[-1].start()
 
+    take(total2.at[others], b2)
+    outs.append(pltpu.make_async_copy(total2, sums_out, outsem.at[NCH]))
+    outs[-1].start()
+    cross = total2[:, size_h:, :].reshape(CROSS, BLOCK)
+    full[:, 0:128] = cross[0:N]
+    full[:, 128:256] = cross[N:2 * N]
+    last = cross[2 * N:2 * N + 152]
+    left = iota((152, BLOCK), 1) < 64
+    full[0:152, 256:384] = jnp.where(left, last, 0.0)
+    full[152:304, 256:384] = jnp.where(left, pltpu.roll(last, 64, 1), 0.0)
+    right[:, 0:N] = nt(full[...], linv[...], HI)
+    right[:, N:] = jnp.zeros((N, LANES - N), F32)
+    outs.append(pltpu.make_async_copy(right, right_out, outsem.at[NCH + 1]))
+    outs[-1].start()
+
     @pl.when(has_down)
     def _():
         for span in SPANS:
             l_copy(*span).wait_recv()
 
-    outs.append(pltpu.make_async_copy(linvp, linvp_out, outsem.at[NCH + 1]))
-    outs[-1].start()
-    each(1, lambda k: all_copy(k).wait_recv())
-    outs.append(pltpu.make_async_copy(total2, sums_out, outsem.at[NCH + 2]))
+    outs.append(pltpu.make_async_copy(linvp, linvp_out, outsem.at[NCH + 2]))
     outs[-1].start()
     for copy in outs:
         copy.wait()
@@ -464,21 +463,18 @@
         for span in SPANS:
             l_copy(*span).wait_send()
 
-    gram_sum.drain()
-
-    def drain(k):
-        h_copy(k).wait_send()
-        all_copy(k).wait_send()
-
-    each(1, drain)
+    take(recv.at[others], a1)
+    take(recv.at[others], a3)
+    take(recv_h.at[others], h1)
+    take(total2.at[others], b1)
 
     @pl.when(z_arrives)
     def _():
-        each(1 - core, lambda k: cross_copy(k).wait_send())
-
-
-def finish_kernel(q_in, sums_in, linv_in, linvp_in, q_out, h_out, c_out, sums, linv, linvp, full, q, sem):
-    pairs = ((q_in, q), (sums_in, sums), (linv_in, linv), (linvp_in, linvp))
+        take_cross(c1)
+
+
+def finish_kernel(q_in, sums_in, right_in, linvp_in, q_out, h_out, c_out, sums, right, linvp, full, q, sem):
+    pairs = ((q_in, q), (sums_in, sums), (right_in, right), (linvp_in, linvp))
     copies = [pltpu.make_async_copy(*pair, sem.at[i]) for i, pair in enumerate(pairs)]
     for copy in copies:
         copy.start()
@@ -487,16 +483,8 @@
     q_copy.start()
     for copy in copies[1:]:
         copy.wait()
-    count, size = sums.shape[0], SYM // sums.shape[0]
-    cross = sums[:, size:, :].reshape(CROSS, BLOCK)
-    full[:, 0:128] = cross[0:N]
-    full[:, 128:256] = cross[N:2 * N]
-    last = cross[2 * N:2 * N + 152]
-    left = iota((152, BLOCK), 1) < 64
-    full[0:152, 256:384] = jnp.where(left, last, 0.0)
-    full[152:304, 256:384] = jnp.where(left, pltpu.roll(last, 64, 1), 0.0)
-    right = nt(full[...], linv[...], HI)
-    c_out[:, 0, :] = nn(linvp[:, 0:N], right, HI)[0:C, 0:C]
+    size = SYM // sums.shape[0]
+    c_out[:, 0, :] = nn(linvp[:, 0:N], right[:, 0:N], HI)[0:C, 0:C]
     b00, b01, b11, b02, b12, b22 = unpack_upper(sums[:, 0:size, :].reshape(SYM, BLOCK))
     full[0:128, 0:128] = b00
     full[0:128, 128:256] = b01
@@ -511,7 +499,7 @@
     q_copy.wait()
 
 
-def finish(q, sums, linv, linvp):
+def finish(q, sums, right, linvp):
     vmem = pl.BlockSpec(memory_space=pltpu.VMEM)
     anywhere = pl.BlockSpec(memory_space=pl.ANY)
     square = jax.ShapeDtypeStruct((C, 1, C), F32)
@@ -521,7 +509,7 @@
         scratch_shapes=[pltpu.VMEM(sums.shape, F32)] + [pltpu.VMEM((N, LANES), F32)] * 3
         + [pltpu.VMEM((C, ROWS), BF16), pltpu.SemaphoreType.DMA((5,))],
         compiler_params=pltpu.CompilerParams(vmem_limit_bytes=57 << 20), name="finish",
-    )(q, sums, linv, linvp)
+    )(q, sums, right, linvp)
 
 
 def shards(x_block, h_diag, h_right, pattern):
@@ -529,7 +517,7 @@
     dma = pltpu.SemaphoreType.DMA
     vmem = pl.BlockSpec(memory_space=pltpu.VMEM)
     rows_b, square, size = (C, ROWS), (ROWS, ROWS), SYM + CROSS
-    q, sums, linv, linvp = pl.pallas_call(
+    q, sums, right, linvp = pl.pallas_call(
         lambda *refs: kernel(count, sectors, *refs),
         out_shape=(jax.ShapeDtypeStruct((C, ROWS), BF16), jax.ShapeDtypeStruct((count, size // count, BLOCK), F32),
                    jax.ShapeDtypeStruct((N, LANES), F32), jax.ShapeDtypeStruct((N, LANES), F32)),
@@ -544,14 +532,14 @@
             pltpu.VMEM((CROSS, BLOCK), F32), pltpu.VMEM((count, CROSS // count, BLOCK), F32),
             pltpu.VMEM((count, size // count, BLOCK), F32),
             pltpu.VMEM((3, N, BLOCK), F32), pltpu.VMEM((N, LANES), F32), pltpu.VMEM((N, LANES), F32),
-            pltpu.VMEM(rows_b, BF16),
+            pltpu.VMEM(rows_b, BF16), pltpu.VMEM((N, LANES), F32),
             dma((1 + 2 * NCH,)), dma((NCH,)), dma((NCH,)), dma((NCH,)), dma((NCH,)), dma((NCH,)), dma((NCH,)),
             dma((3,)), dma((3,)), dma((NCH + 3,)),
-        ] + [dma((count,))] * 10,
+        ] + [dma] * 10,
         compiler_params=pltpu.CompilerParams(collective_id=0, has_side_effects=True, vmem_limit_bytes=57 << 20),
         name="step",
     )(jnp.swapaxes(pattern[0], 0, 1), x_block[0].T, h_diag[0], h_right[0])
-    q, h, corr = finish(q, sums, linv, linvp)
+    q, h, corr = finish(q, sums, right, linvp)
     return q.T[None], jnp.swapaxes(h, 0, 1), jnp.swapaxes(corr, 0, 1)
 
 

time: 65.5 us -> 59 us (0.901)
  the two profiles are of different devices: /device:TPU:135 before, /device:TPU:121 now
where the time goes in v4:
time: 59 us; the launch traced here: 58.8 us
  Pallas kernels  58 us (98%)
  between operations  0.82 us (1%)
    pallas_call x1, Pallas kernels, shards(): pl.pallas_call(lambda *refs: kernel(count, sectors, *refs), out_shape=(ja...  54.2 us
    pallas_call x1, Pallas kernels, finish(): pl.pallas_call(finish_kernel, out_shape=(jax.ShapeDtypeStruct((C, ROWS),...  3.72 us

profile of v4, /device:TPU:121, one launch (start us, length us, event | category | flops | bytes accessed | tf_op | source)
XLA Modules:
  0.0 58.8 jit_solution(16025349607159823734)
XLA Ops:
  0.6 54.2 %step.1 = (bf16[300,1280]{1,0:T(8,128)(2,1)}, f32[32,40,128]{2,1,0:T(8,128)}, f32[304,384]{1,0:T(8,128)}, f32[304,384]{1,0:T(8,128)}) custom-call(s32[10,2,10]{2,1,0:T(2,128)} %bitcast.16, bf16[300,1280]{1,0:T(8,128)(2,1)} %bitcast.15, bf16[1280,1280]{1,0:T(8,128)(2,1)} %bitcast.13, bf16[1280,1280]{1,0:T(8,128)(2,1)} %bitcast.14), custom_call_target="tpu_custom_call" | custom-call | tf_op jit(solution)/shard_map/step/pallas_call | solution.py:520
  54.9 3.7 %finish.1 = (bf16[300,1280]{1,0:T(8,128)(2,1)}, f32[300,1,300]{2,1,0:T(1,128)}, f32[300,1,300]{2,1,0:T(1,128)}) custom-call(bf16[300,1280]{1,0:T(8,128)(2,1)} %get-tuple-element.10.q_in, f32[32,40,128]{2,1,0:T(8,128)} %get-tuple-element.11.sums_in, f32[304,384]{1,0:T(8,128)} %get-tuple-element.12.right_in, f32[304,384]{1,0:T(8,128)} %get-tuple-element.13.linvp_in), custom_call_target="tpu_custom_call" | custom-call | tf_op jit(solution)/shard_map/finish/pallas_call | solution.py:506

commit v5 on v4

--- a/solution.py
+++ b/solution.py
@@ -146,6 +146,10 @@
 SYM = 512
 CROSS = 768
 EARLY = 3
+SIDE = 4
+OFFSETS = sorted(
+    [(dx, dy, dc) for dx in range(SIDE) for dy in range(SIDE) for dc in range(2) if (dx, dy, dc) != (0, 0, 0)],
+    key=lambda d: -(min(d[0], SIDE - d[0]) + min(d[1], SIDE - d[1])))
 SPANS = ((0, 0, 128), (1, 128, 256), (2, 256, 304))
 
 
@@ -292,26 +296,36 @@
     def chunk(index, size):
         return pl.ds(pl.multiple_of(index * size, 8), size)
 
+    along_x = [lax.rem(me // (2 * SIDE) + d, SIDE) * (2 * SIDE) for d in range(SIDE)]
+    along_y = [lax.rem(me // 2 + d, SIDE) * 2 for d in range(SIDE)]
+    along_c = [core, 1 - core]
+
+    def peer_of(k):
+        dx, dy, dc = OFFSETS[k - 1]
+        return along_x[dx] + along_y[dy] + along_c[dc]
+
     def gram_copy(k):
-        peer = lax.rem(me + k, count)
+        peer = peer_of(k)
         return pltpu.make_async_remote_copy(
             src_ref=part.at[chunk(peer, size_h)], dst_ref=recv.at[k], send_sem=a1, recv_sem=a2,
             device_id=(sector, peer), device_id_type=MESH)
 
     def gram_all(k):
-        peer = lax.rem(me + k, count)
+        peer = peer_of(k)
         mine = total.at[chunk(me, size_h)]
         return pltpu.make_async_remote_copy(
             src_ref=mine, dst_ref=mine, send_sem=a3, recv_sem=a4, device_id=(sector, peer), device_id_type=MESH)
 
     others = pl.ds(1, count - 1)
-    each(1, count, lambda k: gram_copy(k).start())
+    for k in range(1, count):
+        gram_copy(k).start()
     recv[0] = part[chunk(me, size_h), :]
     full[0:C, 0:C] = nt(xv[...], yv[...])
     pack_symmetric(full, part_h)
     take(recv.at[others], a2)
     total[chunk(me, size_h), :] = jnp.sum(recv[...], axis=0) * scale
-    each(1, count, lambda k: gram_all(k).start())
+    for k in range(1, count):
+        gram_all(k).start()
 
     def h_copy(k):
         peer = lax.rem(me + k, count)
@@ -326,7 +340,7 @@
             device_id=(sector + core, peer), device_id_type=MESH)
 
     def all_copy(k):
-        peer = lax.rem(me + k, count)
+        peer = peer_of(k)
         return pltpu.make_async_remote_copy(
             src_ref=total2.at[me], dst_ref=total2.at[me], send_sem=b1, recv_sem=b2,
             device_id=(sector, peer), device_id_type=MESH)
@@ -382,7 +396,8 @@
         def _():
             total2[me, size_h:size_h + size_c, :] = jnp.zeros((size_c, BLOCK), F32)
 
-        each(1, count, lambda k: all_copy(k).start())
+        for k in range(1, count):
+            all_copy(k).start()
 
     take(recv.at[others], a4)
     b00, b01, b11, b02, b12, b22 = unpack_upper(total)
@@ -473,18 +488,24 @@
         take_cross(c1)
 
 
-def finish_kernel(q_in, sums_in, right_in, linvp_in, q_out, h_out, c_out, sums, right, linvp, full, q, sem):
-    pairs = ((q_in, q), (sums_in, sums), (right_in, right), (linvp_in, linvp))
+def finish_kernel(q_in, sums_in, right_in, linvp_in, q_out, h_out, c_out, sums, right, linvp, full, h, corr, q, sem, q_sem):
+    pairs = ((sums_in, sums), (right_in, right), (linvp_in, linvp))
     copies = [pltpu.make_async_copy(*pair, sem.at[i]) for i, pair in enumerate(pairs)]
-    for copy in copies:
+
+    def q_copy(source, target, c, way):
+        piece = pl.ds(c * CHUNK, CHUNK)
+        return pltpu.make_async_copy(source.at[:, piece], target.at[:, piece], q_sem.at[way, c])
+
+    copies[0].start()
+    for c in range(NCH):
+        q_copy(q_in, q, c, 0).start()
+    for copy in copies[1:]:
         copy.start()
+    for c in range(NCH):
+        q_copy(q_in, q, c, 0).wait()
+        q_copy(q, q_out, c, 1).start()
     copies[0].wait()
-    q_copy = pltpu.make_async_copy(q, q_out, sem.at[4])
-    q_copy.start()
-    for copy in copies[1:]:
-        copy.wait()
     size = SYM // sums.shape[0]
-    c_out[:, 0, :] = nn(linvp[:, 0:N], right[:, 0:N], HI)[0:C, 0:C]
     b00, b01, b11, b02, b12, b22 = unpack_upper(sums[:, 0:size, :].reshape(SYM, BLOCK))
     full[0:128, 0:128] = b00
     full[0:128, 128:256] = b01
@@ -495,19 +516,29 @@
     full[256:304, 0:128] = b02.T[0:48]
     full[256:304, 128:256] = b12.T[0:48]
     full[256:304, 256:384] = b22
-    h_out[:, 0, :] = full[0:C, 0:C]
-    q_copy.wait()
+    h[:, 0, :] = full[0:C, 0:C]
+    h_copy = pltpu.make_async_copy(h, h_out, sem.at[3])
+    h_copy.start()
+    copies[1].wait()
+    copies[2].wait()
+    corr[:, 0, :] = nn(linvp[:, 0:N], right[:, 0:N], HI)[0:C, 0:C]
+    c_copy = pltpu.make_async_copy(corr, c_out, sem.at[4])
+    c_copy.start()
+    for c in range(NCH):
+        q_copy(q, q_out, c, 1).wait()
+    h_copy.wait()
+    c_copy.wait()
 
 
 def finish(q, sums, right, linvp):
-    vmem = pl.BlockSpec(memory_space=pltpu.VMEM)
     anywhere = pl.BlockSpec(memory_space=pl.ANY)
     square = jax.ShapeDtypeStruct((C, 1, C), F32)
     return pl.pallas_call(
         finish_kernel, out_shape=(jax.ShapeDtypeStruct((C, ROWS), BF16), square, square),
-        in_specs=[anywhere] * 4, out_specs=(anywhere, vmem, vmem),
+        in_specs=[anywhere] * 4, out_specs=(anywhere,) * 3,
         scratch_shapes=[pltpu.VMEM(sums.shape, F32)] + [pltpu.VMEM((N, LANES), F32)] * 3
-        + [pltpu.VMEM((C, ROWS), BF16), pltpu.SemaphoreType.DMA((5,))],
+        + [pltpu.VMEM((C, 1, C), F32)] * 2
+        + [pltpu.VMEM((C, ROWS), BF16), pltpu.SemaphoreType.DMA((5,)), pltpu.SemaphoreType.DMA((2, NCH))],
         compiler_params=pltpu.CompilerParams(vmem_limit_bytes=57 << 20), name="finish",
     )(q, sums, right, linvp)
 

time: 59 us -> 57.6 us (0.976)
  the two profiles are of different devices: /device:TPU:121 before, /device:TPU:97 now
where the time goes in v5:
time: 57.6 us; the launch traced here: 57.4 us
  Pallas kernels  56.6 us (98%)
  between operations  0.8 us (1%)
    pallas_call x1, Pallas kernels, shards(): pl.pallas_call(lambda *refs: kernel(count, sectors, *refs), out_shape=(ja...  52.9 us
    pallas_call x1, Pallas kernels, finish(): pl.pallas_call(finish_kernel, out_shape=(jax.ShapeDtypeStruct((C, ROWS),...  3.73 us

profile of v5, /device:TPU:97, one launch (start us, length us, event | category | flops | bytes accessed | tf_op | source)
XLA Modules:
  0.0 57.4 jit_solution(16074932640092206928)
XLA Ops:
  0.6 52.9 %step.1 = (bf16[300,1280]{1,0:T(8,128)(2,1)}, f32[32,40,128]{2,1,0:T(8,128)}, f32[304,384]{1,0:T(8,128)}, f32[304,384]{1,0:T(8,128)}) custom-call(s32[10,2,10]{2,1,0:T(2,128)} %bitcast.16, bf16[300,1280]{1,0:T(8,128)(2,1)} %bitcast.15, bf16[1280,1280]{1,0:T(8,128)(2,1)} %bitcast.13, bf16[1280,1280]{1,0:T(8,128)(2,1)} %bitcast.14), custom_call_target="tpu_custom_call" | custom-call | tf_op jit(solution)/shard_map/step/pallas_call | solution.py:551
  53.5 3.7 %finish.1 = (bf16[300,1280]{1,0:T(8,128)(2,1)}, f32[300,1,300]{2,1,0:T(1,128)}, f32[300,1,300]{2,1,0:T(1,128)}) custom-call(bf16[300,1280]{1,0:T(8,128)(2,1)} %get-tuple-element.10.q_in, f32[32,40,128]{2,1,0:T(8,128)} %get-tuple-element.11.sums_in, f32[304,384]{1,0:T(8,128)} %get-tuple-element.12.right_in, f32[304,384]{1,0:T(8,128)} %get-tuple-element.13.linvp_in), custom_call_target="tpu_custom_call" | custom-call | tf_op jit(solution)/shard_map/finish/pallas_call | solution.py:536

commit v6 on v5

--- a/solution.py
+++ b/solution.py
@@ -176,19 +176,10 @@
 
     barrier = pltpu.get_barrier_semaphore()
 
-    def signal(k, carry):
-        pl.semaphore_signal(barrier, inc=1, device_id=(sector, lax.rem(me + k, count)), device_id_type=MESH)
-        return carry
-
-    lax.fori_loop(1, count, signal, 0)
-
     @pl.when(has_down)
     def _():
-        def signal_below(k, carry):
+        for k in range(count // 2):
             pl.semaphore_signal(barrier, inc=1, device_id=(sector - 1, 2 * k + 1), device_id_type=MESH)
-            return carry
-
-        lax.fori_loop(0, count // 2, signal_below, 0)
 
     @pl.when(has_down & (core == 0))
     def _():
@@ -197,6 +188,17 @@
     @pl.when(has_up & (core == 1))
     def _():
         pl.semaphore_signal(barrier, inc=1, device_id=(sector + 1, me), device_id_type=MESH)
+
+    along_x = [lax.rem(me // (2 * SIDE) + d, SIDE) * (2 * SIDE) for d in range(SIDE)]
+    along_y = [lax.rem(me // 2 + d, SIDE) * 2 for d in range(SIDE)]
+    along_c = [core, 1 - core]
+
+    def peer_of(k):
+        dx, dy, dc = OFFSETS[k - 1]
+        return along_x[dx] + along_y[dy] + along_c[dc]
+
+    for k in range(1, count):
+        pl.semaphore_signal(barrier, inc=1, device_id=(sector, peer_of(k)), device_id_type=MESH)
 
     above = jnp.where(has_up, jnp.where(core == 1, count, 1), 0)
     below = jnp.where(has_down & (core == 1), 1, 0)
@@ -296,14 +298,6 @@
     def chunk(index, size):
         return pl.ds(pl.multiple_of(index * size, 8), size)
 
-    along_x = [lax.rem(me // (2 * SIDE) + d, SIDE) * (2 * SIDE) for d in range(SIDE)]
-    along_y = [lax.rem(me // 2 + d, SIDE) * 2 for d in range(SIDE)]
-    along_c = [core, 1 - core]
-
-    def peer_of(k):
-        dx, dy, dc = OFFSETS[k - 1]
-        return along_x[dx] + along_y[dy] + along_c[dc]
-
     def gram_copy(k):
         peer = peer_of(k)
         return pltpu.make_async_remote_copy(
@@ -435,6 +429,17 @@
         outs.append(pltpu.make_async_copy(qv.at[:, piece], q_out.at[:, piece], outsem.at[c]))
         outs[-1].start()
 
+    @pl.when(has_down)
+    def _():
+        for span in SPANS[:2]:
+            l_copy(*span).wait_recv()
+
+    def linvp_part(start, stop, index):
+        rows = pl.ds(start, stop - start)
+        outs.append(pltpu.make_async_copy(linvp.at[rows], linvp_out.at[rows], outsem.at[index]))
+        outs[-1].start()
+
+    linvp_part(0, SPANS[1][2], NCH + 2)
     take(total2.at[others], b2)
     outs.append(pltpu.make_async_copy(total2, sums_out, outsem.at[NCH]))
     outs[-1].start()
@@ -452,11 +457,9 @@
 
     @pl.when(has_down)
     def _():
-        for span in SPANS:
-            l_copy(*span).wait_recv()
-
-    outs.append(pltpu.make_async_copy(linvp, linvp_out, outsem.at[NCH + 2]))
-    outs[-1].start()
+        l_copy(*SPANS[2]).wait_recv()
+
+    linvp_part(*SPANS[2][1:], NCH + 3)
     for copy in outs:
         copy.wait()
 
@@ -565,7 +568,7 @@
             pltpu.VMEM((3, N, BLOCK), F32), pltpu.VMEM((N, LANES), F32), pltpu.VMEM((N, LANES), F32),
             pltpu.VMEM(rows_b, BF16), pltpu.VMEM((N, LANES), F32),
             dma((1 + 2 * NCH,)), dma((NCH,)), dma((NCH,)), dma((NCH,)), dma((NCH,)), dma((NCH,)), dma((NCH,)),
-            dma((3,)), dma((3,)), dma((NCH + 3,)),
+            dma((3,)), dma((3,)), dma((NCH + 4,)),
         ] + [dma] * 10,
         compiler_params=pltpu.CompilerParams(collective_id=0, has_side_effects=True, vmem_limit_bytes=57 << 20),
         name="step",

time: 57.6 us -> 56.8 us (0.986)
  Pallas kernels: 56.6 us -> 55.8 us
    pallas_call x1, Pallas kernels: 52.9 us -> 52.1 us  [shards(): pl.pallas_call(lambda *refs: kernel(count, sectors, *refs), out_shape=(ja...]
where the time goes in v6:
time: 56.8 us; the launch traced here: 56.6 us
  Pallas kernels  55.8 us (98%)
  between operations  0.8 us (1%)
    pallas_call x1, Pallas kernels, shards(): pl.pallas_call(lambda *refs: kernel(count, sectors, *refs), out_shape=(ja...  52.1 us
    pallas_call x1, Pallas kernels, finish(): pl.pallas_call(finish_kernel, out_shape=(jax.ShapeDtypeStruct((C, ROWS),...  3.73 us

profile of v6, /device:TPU:97, one launch (start us, length us, event | category | flops | bytes accessed | tf_op | source)
XLA Modules:
  0.0 56.6 jit_solution(914632702530763261)
XLA Ops:
  0.6 52.1 %step.1 = (bf16[300,1280]{1,0:T(8,128)(2,1)}, f32[32,40,128]{2,1,0:T(8,128)}, f32[304,384]{1,0:T(8,128)}, f32[304,384]{1,0:T(8,128)}) custom-call(s32[10,2,10]{2,1,0:T(2,128)} %bitcast.16, bf16[300,1280]{1,0:T(8,128)(2,1)} %bitcast.15, bf16[1280,1280]{1,0:T(8,128)(2,1)} %bitcast.13, bf16[1280,1280]{1,0:T(8,128)(2,1)} %bitcast.14), custom_call_target="tpu_custom_call" | custom-call | tf_op jit(solution)/shard_map/step/pallas_call | solution.py:554
  52.7 3.7 %finish.1 = (bf16[300,1280]{1,0:T(8,128)(2,1)}, f32[300,1,300]{2,1,0:T(1,128)}, f32[300,1,300]{2,1,0:T(1,128)}) custom-call(bf16[300,1280]{1,0:T(8,128)(2,1)} %get-tuple-element.10.q_in, f32[32,40,128]{2,1,0:T(8,128)} %get-tuple-element.11.sums_in, f32[304,384]{1,0:T(8,128)} %get-tuple-element.12.right_in, f32[304,384]{1,0:T(8,128)} %get-tuple-element.13.linvp_in), custom_call_target="tpu_custom_call" | custom-call | tf_op jit(solution)/shard_map/finish/pallas_call | solution.py:539
